TPU v7x, 128 devices: a whole 4x4x4 slice. The times are simulated.
128 devices in a mesh: row: 8 (over z, core), col: 16 (over y, x).
Axes of the slice: x: 4, y: 4, z: 4, core: 2. Of those that a mesh axis runs over, the one named last changes fastest.
Arguments:
- spectral: bfloat16 [3, 2, 5120, 7680], P(None, None, ('row', 'col')), may hold values from -6 to 6
- labels: int32 [2048, 2048], P(('row', 'col')), may hold values from 0 to 16383
- block_place: int32 [128], replicated, may hold values from 0 to 127, each once
Outputs:
- stats: float32 [6, 16, 1024], P(None, 'col', 'row')
Inputs may be any that keep to these rules, and one draw needn't show every extreme that they name: `block_place`: each of 0 to 127 appears once.
All inputs are finite; a program needn't handle non-finite values.
Results may differ from a plain program's by a relative error of at most 0.00073.
Values may be sent and summed in bfloat16 or wider, within the bound.
A program may use at most 192 MiB of HBM per device.

v0:
```python
import math

import jax
import jax.numpy as jnp
from jax import lax
from jax.sharding import PartitionSpec as P

KX = 5120
KZ = 7680
NX = 10240
ZW = 2048
XW = 2048
LB = 128
NBLK = 128


def wave_table(kvals, positions, modulus):
    phase = (kvals * positions % modulus).astype(jnp.float32) * (2.0 * math.pi / modulus)
    return (jnp.cos(phase), jnp.sin(phase))


def column_transform(spectral):
    modes = spectral.shape[2]
    flat = spectral.reshape(6 * modes, KZ)
    kvals = lax.broadcasted_iota(jnp.int32, (KZ, 1), 0)
    width = min(256, ZW)
    pieces = []
    for start in range(0, ZW, width):
        positions = lax.broadcasted_iota(jnp.int32, (1, width), 1) + start
        cosine, sine = wave_table(kvals, positions, KZ)
        pcos = jnp.dot(flat, cosine.astype(jnp.bfloat16), preferred_element_type=jnp.float32)
        psin = jnp.dot(flat, sine.astype(jnp.bfloat16), preferred_element_type=jnp.float32)
        pcos = pcos.reshape(3, 2, modes, width)
        psin = psin.reshape(3, 2, modes, width)
        real_part = pcos[:, 0] - psin[:, 1]
        imag_part = psin[:, 0] + pcos[:, 1]
        pieces.append(jnp.stack([real_part, imag_part], 1).astype(jnp.bfloat16))
    return jnp.concatenate(pieces, 3)


def row_transform(zplane, kx_index):
    kcol = kx_index[:, None]
    weight = jnp.where(kcol == 0, 1.0, 2.0).astype(jnp.float32)
    width = min(512, XW)
    scale = 1.0 / math.sqrt(2.0 * KX * KZ)
    pieces = []
    for start in range(0, XW, width):
        positions = lax.broadcasted_iota(jnp.int32, (1, width), 1) + start
        cosine, sine = wave_table(kcol, positions, NX)
        ctab = (weight * cosine).astype(jnp.bfloat16)
        stab = (weight * sine).astype(jnp.bfloat16)
        value = jnp.einsum("nkz,kx->nzx", zplane[:, 0], ctab, preferred_element_type=jnp.float32)
        value = value - jnp.einsum(
            "nkz,kx->nzx", zplane[:, 1], stab, preferred_element_type=jnp.float32
        )
        pieces.append(value * scale)
    return jnp.concatenate(pieces, 2)


def label_stats(enst, target, zstart, total):
    rows, cols = enst.shape
    zpos = (lax.broadcasted_iota(jnp.int32, (rows, cols), 0) + zstart).astype(jnp.float32) / ZW
    xpos = lax.broadcasted_iota(jnp.int32, (rows, cols), 1).astype(jnp.float32) / XW
    values = jnp.stack(
        [
            jnp.ones_like(enst),
            enst,
            enst * xpos,
            enst * zpos,
            enst * xpos * xpos,
            enst * xpos * zpos,
            enst * zpos * zpos,
        ],
        0,
    )
    table = jnp.zeros((7, total), jnp.float32)
    return table.at[:, target.reshape(-1)].add(values.reshape(7, -1))


def finish(sums):
    weight = jnp.maximum(sums[1], 1.0)
    centre_x = sums[2] / weight
    centre_z = sums[3] / weight
    return jnp.stack(
        [
            sums[1] / jnp.maximum(sums[0], 1.0),
            centre_x,
            centre_z,
            12.0 * (sums[4] / weight - centre_x * centre_x),
            12.0 * (sums[5] / weight - centre_x * centre_z),
            12.0 * (sums[6] / weight - centre_z * centre_z),
        ],
        0,
    )


def on_device(spectral, labels, block_place):
    n_row = lax.axis_size("row")
    n_col = lax.axis_size("col")
    zplane = column_transform(spectral)
    kx_index = lax.broadcasted_iota(jnp.int32, (KX,), 0)
    vort = row_transform(
        lax.all_to_all(zplane, ("row", "col"), split_axis=3, concat_axis=2, tiled=True), kx_index
    )
    enst = jnp.sum(vort * vort, axis=0)
    rows_dev = enst.shape[0]
    row_id = lax.axis_index("row")
    col_id = lax.axis_index("col")
    zstart = (row_id * n_col + col_id) * rows_dev
    target = jnp.take(block_place, labels // LB) * LB + labels % LB
    own_rows = NBLK * LB // n_col
    part_rows = own_rows // n_row
    table = label_stats(enst, target, zstart, NBLK * LB).reshape(7, n_col, own_rows)
    owned = lax.psum_scatter(table, "col", scatter_dimension=1, tiled=True)
    summed = lax.psum_scatter(owned, "row", scatter_dimension=2, tiled=True)
    sums = summed.reshape(7, part_rows)
    return finish(sums).reshape(6, 1, part_rows)


def solution(mesh):
    in_specs = (P(None, None, ("row", "col"), None), P(("row", "col"), None), P())
    out_specs = P(None, "col", "row")
    return jax.shard_map(
        on_device, mesh=mesh, in_specs=in_specs, out_specs=out_specs, check_vma=False
    )
```

profile of v0, /device:TPU:1, one launch (start us, length us, event | category | flops | bytes accessed | tf_op | source)
XLA Modules:
  0.0 1423.3 jit_solution(3410507366284819571)
XLA Ops:
  6.5 36.2 %fusion.88 = f32[256,240]{0,1:T(8,128)S(1)} fusion(bf16[240,7680]{1,0:T(8,128)(2,1)} %bitcast.231), kind=kOutput, calls=%fused_computation.131 | convolution fusion | flops 963379200 | bytes 3932160 | tf_op jit(solution)/shard_map/dot_general | solution.py:31
  42.8 30.6 %fusion.89 = f32[256,240]{0,1:T(8,128)S(1)} fusion(bf16[240,7680]{1,0:T(8,128)(2,1)S(1)} %bitcast.232), kind=kOutput, calls=%fused_computation.132 | convolution fusion | flops 963379200 | bytes 3932160 | tf_op jit(solution)/shard_map/dot_general | solution.py:32
  73.4 42.4 %fusion.91 = f32[256,240]{0,1:T(8,128)S(1)} fusion(bf16[240,7680]{1,0:T(8,128)(2,1)S(1)} %bitcast.233, s32[256]{0:T(256)S(1)} %iota_add_fusion.9), kind=kOutput, calls=%fused_computation.134 | convolution fusion | flops 963379200 | bytes 3933184 | tf_op jit(solution)/shard_map/dot_general | solution.py:32
  146.3 30.6 %fusion.92 = f32[256,240]{0,1:T(8,128)S(1)} fusion(bf16[240,7680]{1,0:T(8,128)(2,1)S(1)} %bitcast.235, s32[256]{0:T(256)S(1)} %iota_add_fusion.8), kind=kOutput, calls=%fused_computation.135 | convolution fusion | flops 963379200 | bytes 3933184 | tf_op jit(solution)/shard_map/dot_general | solution.py:31
  176.9 31.2 %fusion.93 = f32[256,240]{0,1:T(8,128)S(1)} fusion(bf16[240,7680]{1,0:T(8,128)(2,1)S(1)} %bitcast.236, s32[256]{0:T(256)S(1)} %iota_add_fusion.8), kind=kOutput, calls=%fused_computation.136 | convolution fusion | flops 963379200 | bytes 3933184 | tf_op jit(solution)/shard_map/dot_general | solution.py:32
  208.1 30.4 %fusion.94 = f32[256,240]{0,1:T(8,128)S(1)} fusion(bf16[240,7680]{1,0:T(8,128)(2,1)S(1)} %bitcast.237, s32[256]{0:T(256)S(1)} %iota_add_fusion.7), kind=kOutput, calls=%fused_computation.137 | convolution fusion | flops 963379200 | bytes 3933184 | tf_op jit(solution)/shard_map/dot_general | solution.py:31
  238.5 31.2 %fusion.95 = f32[256,240]{0,1:T(8,128)S(1)} fusion(bf16[240,7680]{1,0:T(8,128)(2,1)S(1)} %bitcast.238, s32[256]{0:T(256)S(1)} %iota_add_fusion.7), kind=kOutput, calls=%fused_computation.138 | convolution fusion | flops 963379200 | bytes 3933184 | tf_op jit(solution)/shard_map/dot_general | solution.py:32
  269.8 30.4 %fusion.96 = f32[256,240]{0,1:T(8,128)S(1)} fusion(bf16[240,7680]{1,0:T(8,128)(2,1)S(1)} %bitcast.239, s32[256]{0:T(256)S(1)} %iota_add_fusion.6), kind=kOutput, calls=%fused_computation.139 | convolution fusion | flops 963379200 | bytes 3933184 | tf_op jit(solution)/shard_map/dot_general | solution.py:31
  300.2 31.2 %fusion.97 = f32[256,240]{0,1:T(8,128)S(1)} fusion(bf16[240,7680]{1,0:T(8,128)(2,1)S(1)} %bitcast.240, s32[256]{0:T(256)S(1)} %iota_add_fusion.6), kind=kOutput, calls=%fused_computation.140 | convolution fusion | flops 963379200 | bytes 3933184 | tf_op jit(solution)/shard_map/dot_general | solution.py:32
  331.4 30.4 %fusion.98 = f32[256,240]{0,1:T(8,128)S(1)} fusion(bf16[240,7680]{1,0:T(8,128)(2,1)S(1)} %bitcast.241, s32[256]{0:T(256)S(1)} %iota_add_fusion.5), kind=kOutput, calls=%fused_computation.141 | convolution fusion | flops 963379200 | bytes 3933184 | tf_op jit(solution)/shard_map/dot_general | solution.py:31
  361.9 31.2 %fusion.99 = f32[256,240]{0,1:T(8,128)S(1)} fusion(bf16[240,7680]{1,0:T(8,128)(2,1)S(1)} %bitcast.242, s32[256]{0:T(256)S(1)} %iota_add_fusion.5), kind=kOutput, calls=%fused_computation.142 | convolution fusion | flops 963379200 | bytes 3933184 | tf_op jit(solution)/shard_map/dot_general | solution.py:32
  423.5 31.2 %fusion.101 = f32[256,240]{0,1:T(8,128)S(1)} fusion(bf16[240,7680]{1,0:T(8,128)(2,1)S(1)} %bitcast.244, s32[256]{0:T(256)S(1)} %iota_add_fusion.4), kind=kOutput, calls=%fused_computation.144 | convolution fusion | flops 963379200 | bytes 3933184 | tf_op jit(solution)/shard_map/dot_general | solution.py:32
  485.2 31.2 %fusion.103 = f32[256,240]{0,1:T(8,128)S(1)} fusion(bf16[240,7680]{1,0:T(8,128)(2,1)S(1)} %bitcast.246, s32[256]{0:T(256)S(1)} %iota_add_fusion.3), kind=kOutput, calls=%fused_computation.146 | convolution fusion | flops 963379200 | bytes 3933184 | tf_op jit(solution)/shard_map/dot_general | solution.py:32
  548.4 193.9 %gather_fusion = s32[32768]{0:T(1024)S(1)} fusion(s32[128]{0:T(128)S(1)} %copy-done, s32[32768]{0:T(1024)S(1)} %broadcast_clamp_fusion), kind=kCustom, calls=%fused_computation | custom fusion | bytes 393216 | tf_op jit(solution)/shard_map/jit(_take)/gather | solution.py:110
  763.8 44.4 %fusion.68 = f32[3,16,512]{2,1,0:T(8,128)S(1)} fusion(f32[5120]{0:T(1024)} %fusion.150, bf16[3,2,5120,16]{2,3,0,1:T(8,128)(2,1)} %reshape.497), kind=kOutput, calls=%fused_computation.118 | convolution fusion | flops 280494080 | bytes 610304 | tf_op jit(solution)/shard_map/nkz,kx->nzx/dot_general | solution.py:53
  808.3 42.9 %fusion.125 = f32[3,16,512]{2,1,0:T(8,128)S(1)} fusion(f32[3,16,512]{2,1,0:T(8,128)S(1)} %fusion.68, f32[5120]{0:T(1024)S(1)} %copy-done.3, bf16[3,2,5120,16]{2,3,0,1:T(8,128)(2,1)S(1)} %copy-done.1), kind=kOutput, calls=%fused_computation.154 | convolution fusion | flops 280543232 | bytes 708608 | tf_op jit(solution)/shard_map/nkz,kx->nzx/dot_general | solution.py:52
  851.2 41.1 %fusion.82 = f32[3,16,512]{2,1,0:T(8,128)S(1)} fusion(s32[512]{0:T(512)S(1)} %iota_add_fusion.2, f32[5120]{0:T(1024)S(1)} %copy-done.3, bf16[3,2,5120,16]{2,3,0,1:T(8,128)(2,1)S(1)} %copy-done.1), kind=kOutput, calls=%fused_computation.126 | convolution fusion | flops 280494080 | bytes 612352 | tf_op jit(solution)/shard_map/nkz,kx->nzx/dot_general | solution.py:53
  892.3 40.5 %fusion.107 = f32[3,16,512]{2,1,0:T(8,128)S(1)} fusion(f32[3,16,512]{2,1,0:T(8,128)S(1)} %fusion.82, s32[512]{0:T(512)S(1)} %iota_add_fusion.2, f32[5120]{0:T(1024)S(1)} %copy-done.3, bf16[3,2,5120,16]{2,3,0,1:T(8,128)(2,1)S(1)} %copy-done.1), kind=kOutput, calls=%fused_computation.148 | convolution fusion | flops 280543232 | bytes 710656 | tf_op jit(solution)/shard_map/nkz,kx->nzx/dot_general | solution.py:52
  932.8 40.9 %fusion.78 = f32[3,16,512]{2,1,0:T(8,128)S(1)} fusion(s32[512]{0:T(512)S(1)} %iota_add_fusion.1, f32[5120]{0:T(1024)S(1)} %copy-done.3, bf16[3,2,5120,16]{2,3,0,1:T(8,128)(2,1)S(1)} %copy-done.1), kind=kOutput, calls=%fused_computation.124 | convolution fusion | flops 280494080 | bytes 612352 | tf_op jit(solution)/shard_map/nkz,kx->nzx/dot_general | solution.py:53
  973.7 40.8 %fusion.113 = f32[3,16,512]{2,1,0:T(8,128)S(1)} fusion(f32[3,16,512]{2,1,0:T(8,128)S(1)} %fusion.78, s32[512]{0:T(512)S(1)} %iota_add_fusion.1, f32[5120]{0:T(1024)S(1)} %copy-done.3, bf16[3,2,5120,16]{2,3,0,1:T(8,128)(2,1)S(1)} %copy-done.1), kind=kOutput, calls=%fused_computation.150 | convolution fusion | flops 280543232 | bytes 710656 | tf_op jit(solution)/shard_map/nkz,kx->nzx/dot_general | solution.py:52
  1014.5 40.9 %fusion.74 = f32[3,16,512]{2,1,0:T(8,128)S(1)} fusion(s32[512]{0:T(512)S(1)} %iota_add_fusion, f32[5120]{0:T(1024)S(1)} %copy-done.3, bf16[3,2,5120,16]{2,3,0,1:T(8,128)(2,1)S(1)} %copy-done.1), kind=kOutput, calls=%fused_computation.122 | convolution fusion | flops 280494080 | bytes 612352 | tf_op jit(solution)/shard_map/nkz,kx->nzx/dot_general | solution.py:53
  1055.3 40.6 %fusion.119 = f32[3,16,512]{2,1,0:T(8,128)S(1)} fusion(f32[3,16,512]{2,1,0:T(8,128)S(1)} %fusion.74, s32[512]{0:T(512)S(1)} %iota_add_fusion, f32[5120]{0:T(1024)S(1)} %copy-done.3, bf16[3,2,5120,16]{2,3,0,1:T(8,128)(2,1)S(1)} %copy-done.1), kind=kOutput, calls=%fused_computation.152 | convolution fusion | flops 280543232 | bytes 710656 | tf_op jit(solution)/shard_map/nkz,kx->nzx/dot_general | solution.py:52
  1107.4 177.9 %scatter_custom_fusion = f32[7,16384]{0,1:T(8,128)} fusion(s32[32768]{0:T(1024)S(1)} %bitcast.229, f32[32768,7]{1,0:T(8,128)} %copy.50, f32[]{:T(128)} %constant.118.clone.1), kind=kCustom, calls=%fused_computation.129 | custom fusion | flops 229376 | bytes 459264 | tf_op jit(solution)/shard_map/scatter-add | solution.py:77
  1292.0 83.9 %all-reduce.3.cloned.1.call-done = f32[7,16,1024]{2,1,0:T(8,128)} async-done(((f32[7,16,1024]{2,1,0:T(8,128)}), f32[7,16,1024]{2,1,0:T(8,128)}) %all-reduce.3.cloned.1.call-update) | async-done | bytes 458768
  (95 shorter events, 202.7 us)
Async XLA Ops:
  6.5 541.9 %copy-start = (s32[128]{0:T(128)S(1)}, s32[128]{0:T(128)}, u32[]{:S(2)}) copy-start(s32[128]{0:T(128)} %param.5) | copy-start | bytes 1540
  6.5 36.2 %copy-start.4 = (bf16[3,2,40,7680]{3,2,1,0:T(8,128)(2,1)S(1)}, bf16[3,2,40,7680]{3,2,1,0:T(8,128)(2,1)}, u32[]{:S(2)}) copy-start(bf16[3,2,40,7680]{3,2,1,0:T(8,128)(2,1)} %param.3) | copy-start | bytes 11059204
  517.2 31.0 %copy-start.2 = (s32[16,2048]{1,0:T(8,128)S(1)}, s32[16,2048]{1,0:T(8,128)}, u32[]{:S(2)}) copy-start(s32[16,2048]{1,0:T(8,128)} %param.4) | copy-start | bytes 393220
  536.1 207.6 %all-to-all-start = ((bf16[128,2,1920]{2,1,0:T(2,128)(2,1)}), bf16[128,2,1920]{2,1,0:T(2,128)(2,1)}, u32[]{:S(2)}, u32[]{:S(2)}) async-start(bf16[128,2,1920]{2,1,0:T(2,128)(2,1)} %reshape.502), calls=%async_computation | async-start | bytes 1966080 | tf_op jit(solution)/shard_map/all_to_all | solution.py:103
  548.0 827.8 %all-reduce.3.cloned.1.call-start = ((), (), s32[]{:S(2)}) async-start(), calls=%async_computation.3 | async-start | bytes 917504
  763.8 44.4 %copy-start.1 = (bf16[3,2,5120,16]{2,3,0,1:T(8,128)(2,1)S(1)}, bf16[3,2,5120,16]{2,3,0,1:T(8,128)(2,1)}, u32[]{:S(2)}) copy-start(bf16[3,2,5120,16]{2,3,0,1:T(8,128)(2,1)} %reshape.497) | copy-start | bytes 2949124
  763.8 44.4 %copy-start.3 = (f32[5120]{0:T(1024)S(1)}, f32[5120]{0:T(1024)}, u32[]{:S(2)}) copy-start(f32[5120]{0:T(1024)} %fusion.150) | copy-start | bytes 61444
  1107.4 184.0 %copy-start.5 = (u32[128]{0:T(128)S(1)}, u32[128]{0:T(128)}, u32[]{:S(2)}) copy-start(u32[128]{0:T(128)} %constant.151) | copy-start | bytes 1540
  1291.3 122.1 %reduce-scatter.5.cloned.1.call-start = ((), (), s32[]{:S(2)}) async-start(), calls=%async_computation.2 | async-start | bytes 589824
Sparse Core Ops, SparseCore 0:
  1291.4 84.3 all-reduce.2
  1384.4 28.9 reduce-scatter.4
where the time goes:
time: 1440 us; the launch traced here: 1420 us
  matrix products  842 us (58%)
  local copies, waits for them, and re-layouts  257 us (18%)
  other arithmetic  185 us (13%)
  waiting for transfers between devices  113 us (8%)
  between operations  14.5 us (1%)
    dot_general x8, matrix products, column_transform(): jnp.dot(flat, sine.astype(jnp.bfloat16), preferred_element_type=jnp.float32)  260 us
    dot_general x8, matrix products, column_transform(): jnp.dot(flat, cosine.astype(jnp.bfloat16), preferred_element_type=jnp.flo...  249 us
    gather x2, local copies, waits for them, and re-layouts, on_device(): target = jnp.take(block_place, labels // LB) * LB + labels % LB  194 us
    scatter-add x1, other arithmetic, label_stats(): return table.at[:, target.reshape(-1)].add(values.reshape(7, -1))  178 us
    dot_general x4, matrix products, row_transform(): jnp.einsum('nkz,kx->nzx', zplane[:, 1], stab, preferred_element_type=jnp....  167 us
    dot_general x4, matrix products, row_transform(): jnp.einsum('nkz,kx->nzx', zplane[:, 0], ctab, preferred_element_type=jnp....  165 us
    unnamed x4, waiting for transfers between devices  113 us
    unnamed x33, local copies, waits for them, and re-layouts  29.5 us
  transfers between devices with their start and end apart: 3, of which 2 were waited for; matrix products, arithmetic and copies ran while one was open for 14% of the time, Pallas kernels for 0%

commit v1 on v0

v1 whole, which is shorter than its diff:
```python
import math

import jax
import jax.numpy as jnp
import ml_dtypes
import numpy as np
from jax import lax
from jax.experimental import pallas as pl
from jax.experimental.pallas import tpu as pltpu
from jax.sharding import PartitionSpec as P

KX = 5120
KZ = 7680
NX = 10240
ZW = 2048
XW = 2048
ND = 128
MODES = 40
QK = KZ // 4
ROWS = 16
LANES = 128
NT = (((1,), (1,)), ((), ()))
VMEM_LIMIT = 60 * 1024 * 1024


def split(table):
    high = table.astype(ml_dtypes.bfloat16)
    low = (table - high.astype(np.float64)).astype(ml_dtypes.bfloat16)
    return high, low


def z_table():
    za = np.arange(4)[:, None, None]
    zq = np.arange(4)[None, :, None]
    d = np.arange(ND)[None, None, :]
    z = (16 * d + 4 * zq + za).reshape(4, 512)
    cycle = (np.arange(KZ).astype(np.float32) * np.float32(2.0 * math.pi / KZ)).astype(np.float32)
    cosine = np.cos(cycle).astype(ml_dtypes.bfloat16)
    sine = np.sin(cycle).astype(ml_dtypes.bfloat16)
    phase = (z[:, :, None] * np.arange(QK)[None, None, :]) % KZ
    return np.concatenate([cosine[phase], sine[phase]], 1)


def x_tables():
    s = np.arange(ND)
    xa = np.arange(256)
    angle = 2.0 * math.pi * ((xa[:, None] * s[None, :]) % 256) / 256
    real_rows = np.concatenate([np.cos(angle), -np.sin(angle)], 1)
    imag_rows = np.concatenate([np.sin(angle), np.cos(angle)], 1)
    first = np.stack(split(np.concatenate([real_rows, imag_rows], 0)))
    m = np.zeros(LANES, np.int64)
    m[: 3 * MODES] = np.arange(3 * MODES) % MODES
    angle = 2.0 * math.pi * (xa[:, None] * m[None, :]) / NX
    twiddle = np.stack([np.cos(angle), np.sin(angle)]).astype(np.float32)
    xb = np.arange(8)
    last = np.zeros((3, 8, 2, LANES))
    for c in range(3):
        angle = 2.0 * math.pi * ((xb[:, None] * np.arange(MODES)[None, :]) % MODES) / MODES
        last[c, :, 0, c * MODES : (c + 1) * MODES] = np.cos(angle)
        last[c, :, 1, c * MODES : (c + 1) * MODES] = -np.sin(angle)
    last = last.reshape(24, 2 * LANES)
    high, low = split(last)
    last = np.concatenate([high, low], 0)
    return first, twiddle, last


def z_kernel(spec_ref, tab_ref, out_ref, preal, pimag, high, low):
    za = pl.program_id(0)
    width = 640

    def fill(residue):
        for start in range(0, QK, width):
            reals, imags = [], []
            for c in range(3):
                quarter = [
                    [
                        spec_ref[2 * c + part, :, ka * QK + start : ka * QK + start + width].astype(jnp.float32)
                        for ka in range(4)
                    ]
                    for part in range(2)
                ]
                (r0, r1, r2, r3), (i0, i1, i2, i3) = quarter
                if residue % 2 == 0:
                    pr, pi, qr, qi = r0 + r2, i0 + i2, r1 + r3, i1 + i3
                else:
                    pr, pi, qr, qi = r0 - r2, i0 - i2, r1 - r3, i1 - i3
                if residue == 0:
                    re, im = pr + qr, pi + qi
                elif residue == 1:
                    re, im = pr - qi, pi + qr
                elif residue == 2:
                    re, im = pr - qr, pi - qi
                else:
                    re, im = pr + qi, pi - qr
                reals.append(re)
                imags.append(im)
            pad = jnp.zeros((LANES - 3 * MODES, width), jnp.float32)
            for part, pieces in enumerate((reals, imags)):
                whole = jnp.concatenate(pieces + [pad], 0)
                top = whole.astype(jnp.bfloat16)
                rest = (whole - top.astype(jnp.float32)).astype(jnp.bfloat16)
                high[part * LANES : (part + 1) * LANES, start : start + width] = top
                low[part * LANES : (part + 1) * LANES, start : start + width] = rest

    for residue in range(4):
        pl.when(za == residue)(lambda residue=residue: fill(residue))

    for zq in range(4):
        sums = []
        for part in range(2):
            rows = tab_ref[0, part * 512 + zq * ND : part * 512 + (zq + 1) * ND, :]
            sums.append(
                lax.dot_general(rows, high[...], NT, preferred_element_type=jnp.float32)
                + lax.dot_general(rows, low[...], NT, preferred_element_type=jnp.float32)
            )
        cosine, sine = sums
        real = cosine[:, :LANES] - sine[:, LANES:]
        imag = sine[:, :LANES] + cosine[:, LANES:]
        preal[pl.ds(za * 4 + zq, ND, stride=ROWS), :] = real
        pimag[pl.ds(za * 4 + zq, ND, stride=ROWS), :] = imag

    @pl.when(za == 3)
    def _():
        out_ref[:, :LANES] = preal[...].astype(jnp.bfloat16)
        out_ref[:, LANES:] = pimag[...].astype(jnp.bfloat16)


def z_transform(spec, table):
    return pl.pallas_call(
        z_kernel,
        out_shape=jax.ShapeDtypeStruct((ND * ROWS, 2 * LANES), jnp.bfloat16),
        grid=(4,),
        in_specs=[
            pl.BlockSpec((6, MODES, KZ), lambda i: (0, 0, 0)),
            pl.BlockSpec((1, 1024, QK), lambda i: (i, 0, 0)),
        ],
        out_specs=pl.BlockSpec((ND * ROWS, 2 * LANES), lambda i: (0, 0)),
        scratch_shapes=[
            pltpu.VMEM((ND * ROWS, LANES), jnp.float32),
            pltpu.VMEM((ND * ROWS, LANES), jnp.float32),
            pltpu.VMEM((2 * LANES, QK), jnp.bfloat16),
            pltpu.VMEM((2 * LANES, QK), jnp.bfloat16),
        ],
        compiler_params=pltpu.CompilerParams(vmem_limit_bytes=VMEM_LIMIT),
    )(spec, table)


def zpoint(i):
    return 4 * (i % 4) + i // 4


def x_kernel(me_ref, place_ref, recv_ref, lab_ref, first_ref, tw_ref, last_ref, out_ref, wreal, wimag, enst, acc0, acc1, lhs, rhs):
    scale = 2.0 / math.sqrt(2.0 * KX * KZ)
    wreal[...] = recv_ref[:, :LANES].astype(jnp.float32)
    wimag[...] = recv_ref[:, LANES:].astype(jnp.float32)
    lane = lax.broadcasted_iota(jnp.int32, (ROWS, LANES), 1)
    factor = jnp.where((lane == 0) | (lane == MODES) | (lane == 2 * MODES), 0.5, 1.0)
    wreal[0:ROWS, :] = wreal[0:ROWS, :] * factor
    wimag[0:ROWS, :] = wimag[0:ROWS, :] * factor

    def transform(pair, carry):
        sides = []
        for half in range(2):
            rows = pl.ds(pair * 2 + half, ND, stride=ROWS)
            sides.append(jnp.concatenate([wreal[rows, :], wimag[rows, :]], 0))
        both = jnp.concatenate(sides, 1).astype(jnp.bfloat16)
        y = jnp.dot(first_ref[0], both, preferred_element_type=jnp.float32) + jnp.dot(
            first_ref[1], both, preferred_element_type=jnp.float32
        )
        cosine, sine = tw_ref[0], tw_ref[1]
        for half in range(2):
            yr = y[0:256, half * LANES : (half + 1) * LANES]
            yi = y[256:512, half * LANES : (half + 1) * LANES]
            t = jnp.concatenate([yr * cosine - yi * sine, yr * sine + yi * cosine], 1)
            top = t.astype(jnp.bfloat16)
            rest = (t - top.astype(jnp.float32)).astype(jnp.bfloat16)
            v = lax.dot_general(last_ref[...], top, NT, preferred_element_type=jnp.float32)
            v = v[0:24] + v[24:48]
            v = v + lax.dot_general(last_ref[0:24], rest, NT, preferred_element_type=jnp.float32)
            v = v * scale
            enst[pair * 2 + half] = v[0:8] * v[0:8] + v[8:16] * v[8:16] + v[16:24] * v[16:24]
        return carry

    lax.fori_loop(0, ROWS // 2, transform, 0)

    acc0[...] = jnp.zeros_like(acc0)
    acc1[...] = jnp.zeros_like(acc1)
    upos = (
        lax.broadcasted_iota(jnp.int32, (8, 256), 0) * 256 + lax.broadcasted_iota(jnp.int32, (8, 256), 1)
    ).astype(jnp.float32) / XW - 0.5
    row64 = lax.broadcasted_iota(jnp.int32, (64, 256), 0)
    row256 = lax.broadcasted_iota(jnp.int32, (256, 256), 0)

    def gather(i, carry):
        z = zpoint(i)
        e = enst[i]
        ehigh = e.astype(jnp.bfloat16).astype(jnp.float32)
        eu = e * upos
        values = [jnp.ones_like(e), ehigh, e - ehigh, eu, eu * upos]
        for xb in range(8):
            cols = slice(xb * 256, (xb + 1) * 256)
            lab = lab_ref[pl.ds(z, 1), cols]
            hit = jnp.broadcast_to(lab >> 8, (64, 256)) == row64
            for j, value in enumerate(values):
                picked = jnp.where(hit, jnp.broadcast_to(value[xb : xb + 1], (64, 256)), 0.0)
                lhs[j * 64 : (j + 1) * 64, cols] = picked.astype(jnp.bfloat16)
            near = jnp.broadcast_to(lab & 255, (256, 256)) == row256
            rhs[:, cols] = jnp.where(near, 1.0, 0.0).astype(jnp.bfloat16)
        t = lax.dot_general(lhs[...], rhs[...], NT, preferred_element_type=jnp.float32)
        w = (me_ref[0] * ROWS + z).astype(jnp.float32) / ZW - 0.5
        e_sum = t[64:128] + t[128:192]
        eu_sum = t[192:256]
        terms = [t[0:64], e_sum, eu_sum, e_sum * w, t[256:320], eu_sum * w, e_sum * (w * w)]
        for j, term in enumerate(terms):
            acc0[j * 64 : (j + 1) * 64, :] += term[:, :128]
            acc1[j * 64 : (j + 1) * 64, :] += term[:, 128:]
        return carry

    lax.fori_loop(0, ROWS, gather, 0)

    for b in range(128):
        place = place_ref[b]
        owner = (place % 8) * 16 + place // 8
        out_ref[owner] = (acc0, acc1)[b % 2][pl.ds(b // 2, 8, stride=64), :]


def x_transform(me, place, recv, labels, first, twiddle, last):
    vmem = pl.BlockSpec(memory_space=pltpu.VMEM)
    smem = pl.BlockSpec(memory_space=pltpu.SMEM)
    return pl.pallas_call(
        x_kernel,
        out_shape=jax.ShapeDtypeStruct((ND, 8, 128), jnp.float32),
        in_specs=[smem, smem, vmem, vmem, vmem, vmem, vmem],
        out_specs=vmem,
        scratch_shapes=[
            pltpu.VMEM((ND * ROWS, LANES), jnp.float32),
            pltpu.VMEM((ND * ROWS, LANES), jnp.float32),
            pltpu.VMEM((ROWS, 8, 256), jnp.float32),
            pltpu.VMEM((512, 128), jnp.float32),
            pltpu.VMEM((512, 128), jnp.float32),
            pltpu.VMEM((320, XW), jnp.bfloat16),
            pltpu.VMEM((256, XW), jnp.bfloat16),
        ],
        compiler_params=pltpu.CompilerParams(vmem_limit_bytes=VMEM_LIMIT),
    )(me, place, recv, labels, first, twiddle, last)


def finish(centred):
    count, s1, u1, w1, uu, uw, ww = (centred[j] for j in range(7))
    s2 = u1 + 0.5 * s1
    s3 = w1 + 0.5 * s1
    s4 = uu + u1 + 0.25 * s1
    s5 = uw + 0.5 * (u1 + w1) + 0.25 * s1
    s6 = ww + w1 + 0.25 * s1
    weight = jnp.maximum(s1, 1.0)
    centre_x = s2 / weight
    centre_z = s3 / weight
    return jnp.stack(
        [
            s1 / jnp.maximum(count, 1.0),
            centre_x,
            centre_z,
            12.0 * (s4 / weight - centre_x * centre_x),
            12.0 * (s5 / weight - centre_x * centre_z),
            12.0 * (s6 / weight - centre_z * centre_z),
        ],
        0,
    )


def solution(mesh):
    table = z_table()
    first, twiddle, last = x_tables()

    def on_device(spectral, labels, block_place):
        me = lax.axis_index("row") * lax.axis_size("col") + lax.axis_index("col")
        msg = z_transform(spectral.reshape(6, MODES, KZ), table)
        msg = msg.reshape(ND, ROWS, 2 * LANES)
        recv = lax.all_to_all(msg, ("row", "col"), split_axis=0, concat_axis=0, tiled=True)
        sums = x_transform(
            me.reshape(1), block_place, recv.reshape(ND * ROWS, 2 * LANES), labels, first, twiddle, last
        )
        parts = lax.all_to_all(sums, ("row", "col"), split_axis=0, concat_axis=0, tiled=True)
        return finish(jnp.sum(parts, axis=0)).reshape(6, 1, 128)

    in_specs = (P(None, None, ("row", "col"), None), P(("row", "col"), None), P())
    return jax.shard_map(on_device, mesh=mesh, in_specs=in_specs, out_specs=P(None, "col", "row"), check_vma=False)
```

time: 1440 us -> 97.4 us (0.07); the launches traced: 1420 us -> 97.2 us
  matrix products: 842 us -> 0 us
  local copies, waits for them, and re-layouts: 257 us -> 1.58 us
  other arithmetic: 185 us -> 0.17 us
  waiting for transfers between devices: 113 us -> 18.8 us
  Pallas kernels: 0 us -> 46.1 us
  blocking collectives: 0 us -> 19 us
  between operations: 14.5 us -> 0.03 us
    dot_general x24 -> x0, matrix products: 842 us -> none  [the longest x8 260 us: column_transform(): jnp.dot(flat, sine.astype(jnp.bfloat16), preferred_element_type=jnp.float32)]
    gather x2 -> x0, local copies, waits for them, and re-layouts: 194 us -> none  [on_device(): target = jnp.take(block_place, labels // LB) * LB + labels % LB]
    scatter-add x1 -> x0, other arithmetic: 178 us -> none  [label_stats(): return table.at[:, target.reshape(-1)].add(values.reshape(7, -1))]
    unnamed x4 -> x0, waiting for transfers between devices: 113 us -> none
    pallas_call x0 -> x2, Pallas kernels: none -> 46.1 us  [the longest x1 27.6 us: z_transform(): pl.pallas_call(z_kernel, out_shape=jax.ShapeDtypeStruct((ND * ROWS, 2 * L...]
    unnamed x33 -> x2, local copies, waits for them, and re-layouts: 29.5 us -> 0.97 us
    all_to_all x0 -> x1, blocking collectives: none -> 19 us  [on_device(): lax.all_to_all(sums, ('row', 'col'), split_axis=0, concat_axis=0, tiled=T...]
    all_to_all x1, waiting for transfers between devices: 0.01 us -> 18.8 us  [on_device(): lax.all_to_all(msg, ('row', 'col'), split_axis=0, concat_axis=0, tiled=True)]
  transfers between devices with their start and end apart: 3 -> 1, of which waited for: 2 -> 1; matrix products, arithmetic and copies ran while one was open for 14% -> 0% of each run, Pallas kernels for 0% -> 0%
where the time goes in v1:
time: 97.4 us; the launch traced here: 97.2 us
  Pallas kernels  46.1 us (47%)
  blocking collectives  19 us (20%)
  waiting for transfers between devices  18.8 us (19%)
  starting transfers between devices  11.5 us (12%)
  local copies, waits for them, and re-layouts  1.58 us (2%)
    pallas_call x1, Pallas kernels, z_transform(): pl.pallas_call(z_kernel, out_shape=jax.ShapeDtypeStruct((ND * ROWS, 2 * L...  27.6 us
    all_to_all x1, blocking collectives, on_device(): lax.all_to_all(sums, ('row', 'col'), split_axis=0, concat_axis=0, tiled=T...  19 us
    all_to_all x1, waiting for transfers between devices, on_device(): lax.all_to_all(msg, ('row', 'col'), split_axis=0, concat_axis=0, tiled=True)  18.8 us
    pallas_call x1, Pallas kernels, x_transform(): pl.pallas_call(x_kernel, out_shape=jax.ShapeDtypeStruct((ND, 8, 128), jnp...  18.5 us
    all_to_all x1, starting transfers between devices, on_device(): lax.all_to_all(msg, ('row', 'col'), split_axis=0, concat_axis=0, tiled=True)  11.5 us
  transfers between devices with their start and end apart: 1, of which 1 were waited for; matrix products, arithmetic and copies ran while one was open for 0% of the time, Pallas kernels for 0%

profile of v1, /device:TPU:1, one launch (start us, length us, event | category | flops | bytes accessed | tf_op | source)
XLA Modules:
  0.0 97.2 jit_solution(5262234848096995639)
XLA Ops:
  0.0 27.6 %shard_map.73 = bf16[2048,256]{1,0:T(8,128)(2,1)} custom-call(bf16[6,40,7680]{2,1,0:T(8,128)(2,1)} %bitcast.6, bf16[4,1024,1920]{2,1,0:T(8,128)(2,1)} %constant.29.clone.tab_ref), custom_call_target="tpu_custom_call" | custom-call | tf_op jit(solution)/shard_map/pallas_call | solution.py:129
  27.6 11.5 %all-to-all-start = ((bf16[128,16,256]{2,1,0:T(8,128)(2,1)}), bf16[128,16,256]{2,1,0:T(8,128)(2,1)S(1)}, u32[]{:S(2)}, u32[]{:S(2)}) async-start(bf16[128,16,256]{2,1,0:T(8,128)(2,1)} %bitcast.4), calls=%async_computation | async-start | bytes 2097152 | tf_op jit(solution)/shard_map/all_to_all | solution.py:279
  39.1 18.8 %all-to-all-done = bf16[128,16,256]{2,1,0:T(8,128)(2,1)S(1)} async-done(((bf16[128,16,256]{2,1,0:T(8,128)(2,1)}), bf16[128,16,256]{2,1,0:T(8,128)(2,1)S(1)}, u32[]{:S(2)}, u32[]{:S(2)}) %all-to-all-start) | async-done | bytes 1048608 | tf_op jit(solution)/shard_map/all_to_all | solution.py:279
  57.9 0.0 copy-start
  57.9 1.0 copy-done
  58.8 18.5 %shard_map.74 = f32[128,8,128]{2,1,0:T(8,128)} custom-call(s32[1]{0:T(128)} %bitcast.me_ref, s32[128]{0:T(128)} %place_ref.1, bf16[2048,256]{1,0:T(8,128)(2,1)} %bitcast.5, s32[16,2048]{1,0:T(8,128)} %lab_ref.1, bf16[2,512,256]{2,1,0:T(8,128)(2,1)} %constant.30.clone.first_ref, f32[2,256,128]{2,1,0:T(8,128)} %constant.31.clone.tw_ref, ...), custom_call_target="tpu_custom_call" | custom-call | tf_op jit(solution)/shard_map/pallas_call | solution.py:230
  77.4 19.0 %all_to_all.10 = f32[128,8,128]{2,1,0:T(8,128)S(1)} all-to-all(f32[128,8,128]{2,1,0:T(8,128)} %shard_map.74), channel_id=1, replica_groups=mesh['row'=8,'col'=16] {'row','col'}, dimensions={0} | all-to-all | bytes 1048576 | tf_op jit(solution)/shard_map/all_to_all | solution.py:283
  96.4 0.1 reduce_sum.9
  96.6 0.6 reshape.19
  (4 shorter events, 0.1 us)
Async XLA Ops:
  27.6 30.3 %all-to-all-start = ((bf16[128,16,256]{2,1,0:T(8,128)(2,1)}), bf16[128,16,256]{2,1,0:T(8,128)(2,1)S(1)}, u32[]{:S(2)}, u32[]{:S(2)}) async-start(bf16[128,16,256]{2,1,0:T(8,128)(2,1)} %bitcast.4), calls=%async_computation | async-start | bytes 2097152 | tf_op jit(solution)/shard_map/all_to_all | solution.py:279
  57.9 1.0 copy-start

commit v2 on v1

--- a/solution.py
+++ b/solution.py
@@ -19,6 +19,7 @@
 QK = KZ // 4
 ROWS = 16
 LANES = 128
+MESH = pl.DeviceIdType.MESH
 NT = (((1,), (1,)), ((), ()))
 VMEM_LIMIT = 60 * 1024 * 1024
 
@@ -47,7 +48,7 @@
     angle = 2.0 * math.pi * ((xa[:, None] * s[None, :]) % 256) / 256
     real_rows = np.concatenate([np.cos(angle), -np.sin(angle)], 1)
     imag_rows = np.concatenate([np.sin(angle), np.cos(angle)], 1)
-    first = np.stack(split(np.concatenate([real_rows, imag_rows], 0)))
+    first = np.concatenate(split(np.concatenate([real_rows, imag_rows], 0)), 1)
     m = np.zeros(LANES, np.int64)
     m[: 3 * MODES] = np.arange(3 * MODES) % MODES
     angle = 2.0 * math.pi * (xa[:, None] * m[None, :]) / NX
@@ -149,7 +150,15 @@
     return 4 * (i % 4) + i // 4
 
 
-def x_kernel(me_ref, place_ref, recv_ref, lab_ref, first_ref, tw_ref, last_ref, out_ref, wreal, wimag, enst, acc0, acc1, lhs, rhs):
+def spread(row, count):
+    tile = jnp.broadcast_to(row, (16, row.shape[1])).astype(jnp.bfloat16)
+    return jnp.concatenate([tile] * (count // 16), 0)
+
+
+def x_kernel(
+    me_ref, place_ref, recv_ref, lab_ref, first_ref, tw_ref, last_ref, out_ref,
+    wreal, wimag, mats, top, rest, enst, acc0, acc1, lhs_a, rhs_a, lhs_b, rhs_b,
+):
     scale = 2.0 / math.sqrt(2.0 * KX * KZ)
     wreal[...] = recv_ref[:, :LANES].astype(jnp.float32)
     wimag[...] = recv_ref[:, LANES:].astype(jnp.float32)
@@ -157,70 +166,82 @@
     factor = jnp.where((lane == 0) | (lane == MODES) | (lane == 2 * MODES), 0.5, 1.0)
     wreal[0:ROWS, :] = wreal[0:ROWS, :] * factor
     wimag[0:ROWS, :] = wimag[0:ROWS, :] * factor
-
-    def transform(pair, carry):
-        sides = []
-        for half in range(2):
-            rows = pl.ds(pair * 2 + half, ND, stride=ROWS)
-            sides.append(jnp.concatenate([wreal[rows, :], wimag[rows, :]], 0))
-        both = jnp.concatenate(sides, 1).astype(jnp.bfloat16)
-        y = jnp.dot(first_ref[0], both, preferred_element_type=jnp.float32) + jnp.dot(
-            first_ref[1], both, preferred_element_type=jnp.float32
-        )
-        cosine, sine = tw_ref[0], tw_ref[1]
+    for i in range(ROWS):
+        rows = pl.ds(i, ND, stride=ROWS)
+        cols = slice(i * LANES, (i + 1) * LANES)
+        for part, wide in enumerate((wreal, wimag)):
+            mat = wide[rows, :].astype(jnp.bfloat16)
+            mats[part * ND : (part + 1) * ND, cols] = mat
+            mats[(part + 2) * ND : (part + 3) * ND, cols] = mat
+
+    cosine, sine = tw_ref[0], tw_ref[1]
+    for pair in range(ROWS // 2):
+        both = mats[:, pair * 256 : (pair + 1) * 256]
+        y = jnp.dot(first_ref[...], both, preferred_element_type=jnp.float32)
         for half in range(2):
             yr = y[0:256, half * LANES : (half + 1) * LANES]
             yi = y[256:512, half * LANES : (half + 1) * LANES]
             t = jnp.concatenate([yr * cosine - yi * sine, yr * sine + yi * cosine], 1)
-            top = t.astype(jnp.bfloat16)
-            rest = (t - top.astype(jnp.float32)).astype(jnp.bfloat16)
-            v = lax.dot_general(last_ref[...], top, NT, preferred_element_type=jnp.float32)
-            v = v[0:24] + v[24:48]
-            v = v + lax.dot_general(last_ref[0:24], rest, NT, preferred_element_type=jnp.float32)
-            v = v * scale
-            enst[pair * 2 + half] = v[0:8] * v[0:8] + v[8:16] * v[8:16] + v[16:24] * v[16:24]
-        return carry
-
-    lax.fori_loop(0, ROWS // 2, transform, 0)
+            high = t.astype(jnp.bfloat16)
+            rows = slice((pair * 2 + half) * 256, (pair * 2 + half + 1) * 256)
+            top[rows, :] = high
+            rest[rows, :] = (t - high.astype(jnp.float32)).astype(jnp.bfloat16)
+    v = lax.dot_general(last_ref[...], top[...], NT, preferred_element_type=jnp.float32)
+    v = v[0:24] + v[24:48]
+    v = v + lax.dot_general(last_ref[0:24], rest[...], NT, preferred_element_type=jnp.float32)
+    v = v * scale
+    enst[...] = v[0:8] * v[0:8] + v[8:16] * v[8:16] + v[16:24] * v[16:24]
 
     acc0[...] = jnp.zeros_like(acc0)
     acc1[...] = jnp.zeros_like(acc1)
     upos = (
         lax.broadcasted_iota(jnp.int32, (8, 256), 0) * 256 + lax.broadcasted_iota(jnp.int32, (8, 256), 1)
     ).astype(jnp.float32) / XW - 0.5
-    row64 = lax.broadcasted_iota(jnp.int32, (64, 256), 0)
-    row256 = lax.broadcasted_iota(jnp.int32, (256, 256), 0)
-
-    def gather(i, carry):
+    row64 = lax.broadcasted_iota(jnp.int32, (64, 256), 0).astype(jnp.float32).astype(jnp.bfloat16)
+    row256 = lax.broadcasted_iota(jnp.int32, (256, 256), 0).astype(jnp.float32).astype(jnp.bfloat16)
+    one = jnp.ones((), jnp.bfloat16)
+    zero = jnp.zeros((), jnp.bfloat16)
+
+    def build(i, lhs, rhs):
         z = zpoint(i)
-        e = enst[i]
+        e = enst[:, pl.ds(pl.multiple_of(i * 256, 256), 256)]
         ehigh = e.astype(jnp.bfloat16).astype(jnp.float32)
         eu = e * upos
-        values = [jnp.ones_like(e), ehigh, e - ehigh, eu, eu * upos]
+        values = [ehigh, e - ehigh, eu, eu * upos]
         for xb in range(8):
             cols = slice(xb * 256, (xb + 1) * 256)
             lab = lab_ref[pl.ds(z, 1), cols]
-            hit = jnp.broadcast_to(lab >> 8, (64, 256)) == row64
+            hit = spread((lab >> 8).astype(jnp.float32), 64) == row64
+            lhs[0:64, cols] = jnp.where(hit, one, zero)
             for j, value in enumerate(values):
-                picked = jnp.where(hit, jnp.broadcast_to(value[xb : xb + 1], (64, 256)), 0.0)
-                lhs[j * 64 : (j + 1) * 64, cols] = picked.astype(jnp.bfloat16)
-            near = jnp.broadcast_to(lab & 255, (256, 256)) == row256
-            rhs[:, cols] = jnp.where(near, 1.0, 0.0).astype(jnp.bfloat16)
+                lhs[(j + 1) * 64 : (j + 2) * 64, cols] = jnp.where(hit, spread(value[xb : xb + 1], 64), zero)
+            near = spread((lab & 255).astype(jnp.float32), 256) == row256
+            rhs[:, cols] = jnp.where(near, one, zero)
+
+    def collect(i, lhs, rhs):
         t = lax.dot_general(lhs[...], rhs[...], NT, preferred_element_type=jnp.float32)
-        w = (me_ref[0] * ROWS + z).astype(jnp.float32) / ZW - 0.5
+        w = (me_ref[0] * ROWS + zpoint(i)).astype(jnp.float32) / ZW - 0.5
         e_sum = t[64:128] + t[128:192]
         eu_sum = t[192:256]
         terms = [t[0:64], e_sum, eu_sum, e_sum * w, t[256:320], eu_sum * w, e_sum * (w * w)]
         for j, term in enumerate(terms):
             acc0[j * 64 : (j + 1) * 64, :] += term[:, :128]
             acc1[j * 64 : (j + 1) * 64, :] += term[:, 128:]
+
+    build(0, lhs_a, rhs_a)
+
+    def two_rows(n, carry):
+        build(2 * n + 1, lhs_b, rhs_b)
+        collect(2 * n, lhs_a, rhs_a)
+        build(lax.rem(2 * n + 2, ROWS), lhs_a, rhs_a)
+        collect(2 * n + 1, lhs_b, rhs_b)
         return carry
 
-    lax.fori_loop(0, ROWS, gather, 0)
+    lax.fori_loop(0, ROWS // 2, two_rows, 0)
 
     for b in range(128):
         place = place_ref[b]
-        owner = (place % 8) * 16 + place // 8
+        owner = (place % 2) * 64 + (place % 8) // 2 * 16 + place // 8
         out_ref[owner] = (acc0, acc1)[b % 2][pl.ds(b // 2, 8, stride=64), :]
 
 
@@ -235,14 +256,87 @@
         scratch_shapes=[
             pltpu.VMEM((ND * ROWS, LANES), jnp.float32),
             pltpu.VMEM((ND * ROWS, LANES), jnp.float32),
-            pltpu.VMEM((ROWS, 8, 256), jnp.float32),
+            pltpu.VMEM((512, ROWS * LANES), jnp.bfloat16),
+            pltpu.VMEM((ROWS * 256, 2 * LANES), jnp.bfloat16),
+            pltpu.VMEM((ROWS * 256, 2 * LANES), jnp.bfloat16),
+            pltpu.VMEM((8, ROWS * 256), jnp.float32),
             pltpu.VMEM((512, 128), jnp.float32),
             pltpu.VMEM((512, 128), jnp.float32),
+            pltpu.VMEM((320, XW), jnp.bfloat16),
+            pltpu.VMEM((256, XW), jnp.bfloat16),
             pltpu.VMEM((320, XW), jnp.bfloat16),
             pltpu.VMEM((256, XW), jnp.bfloat16),
         ],
         compiler_params=pltpu.CompilerParams(vmem_limit_bytes=VMEM_LIMIT),
     )(me, place, recv, labels, first, twiddle, last)
+
+
+def owner_of(core, q):
+    return (q // 16 * 2 + core, q % 16)
+
+
+def sum_kernel(sums_ref, out_ref, mate, part, parts, pair_send, pair_recv, send_sem, recv_sem):
+    row = lax.axis_index("row")
+    col = lax.axis_index("col")
+    core = row % 2
+    mine = row // 2 * 16 + col
+    barrier = pltpu.get_barrier_semaphore()
+    other = (row + 1 - 2 * core, col)
+    pl.semaphore_signal(barrier, inc=1, device_id=other, device_id_type=MESH)
+
+    def greet(j, carry):
+        pl.semaphore_signal(barrier, inc=1, device_id=owner_of(core, lax.rem(mine + j, 64)), device_id_type=MESH)
+        return carry
+
+    lax.fori_loop(1, 64, greet, 0)
+    pl.semaphore_wait(barrier, 64)
+    swap = pltpu.make_async_remote_copy(
+        src_ref=sums_ref.at[pl.ds((1 - core) * 64, 64)],
+        dst_ref=mate,
+        send_sem=pair_send,
+        recv_sem=pair_recv,
+        device_id=other,
+        device_id_type=MESH,
+    )
+    swap.start()
+    swap.wait()
+    part[...] = sums_ref[pl.ds(core * 64, 64)] + mate[...]
+
+    def send(j, carry):
+        q = lax.rem(mine + j, 64)
+        pltpu.make_async_remote_copy(
+            src_ref=part.at[q],
+            dst_ref=parts.at[mine],
+            send_sem=send_sem,
+            recv_sem=recv_sem,
+            device_id=owner_of(core, q),
+            device_id_type=MESH,
+        ).start()
+        return carry
+
+    lax.fori_loop(1, 64, send, 0)
+    parts[mine] = part[mine]
+    every = parts.at[pl.ds(0, 63)]
+    pltpu.make_async_copy(part.at[pl.ds(0, 63)], every, send_sem).wait()
+    pltpu.make_async_copy(every, every, recv_sem).wait()
+    out_ref[...] = finish(jnp.sum(parts[...], 0))
+
+
+def sum_up(sums):
+    vmem = pl.BlockSpec(memory_space=pltpu.VMEM)
+    return pl.pallas_call(
+        sum_kernel,
+        out_shape=jax.ShapeDtypeStruct((6, 128), jnp.float32),
+        in_specs=[vmem],
+        out_specs=vmem,
+        scratch_shapes=[
+            pltpu.VMEM((64, 8, 128), jnp.float32),
+            pltpu.VMEM((64, 8, 128), jnp.float32),
+            pltpu.VMEM((64, 8, 128), jnp.float32),
+        ]
+        + [pltpu.SemaphoreType.DMA] * 4,
+        compiler_params=pltpu.CompilerParams(collective_id=1, has_side_effects=True),
+    )(sums)
 
 
 def finish(centred):
@@ -280,8 +374,7 @@
         sums = x_transform(
             me.reshape(1), block_place, recv.reshape(ND * ROWS, 2 * LANES), labels, first, twiddle, last
         )
-        parts = lax.all_to_all(sums, ("row", "col"), split_axis=0, concat_axis=0, tiled=True)
-        return finish(jnp.sum(parts, axis=0)).reshape(6, 1, 128)
+        return sum_up(sums).reshape(6, 1, 128)
 
     in_specs = (P(None, None, ("row", "col"), None), P(("row", "col"), None), P())
     return jax.shard_map(on_device, mesh=mesh, in_specs=in_specs, out_specs=P(None, "col", "row"), check_vma=False)

time: 97.4 us -> 89.6 us (0.920)
  blocking collectives: 19 us -> 0 us
  Pallas kernels: 46.1 us -> 56.8 us
    all_to_all x1 -> x0, blocking collectives: 19 us -> none  [on_device(): lax.all_to_all(sums, ('row', 'col'), split_axis=0, concat_axis=0, tiled=T...]
    pallas_call x0 -> x1, Pallas kernels: none -> 14.5 us  [sum_up(): pl.pallas_call(sum_kernel, out_shape=jax.ShapeDtypeStruct((6, 128), jnp.f...]
    pallas_call x1, Pallas kernels: 18.5 us -> 14.7 us  [x_transform(): pl.pallas_call(x_kernel, out_shape=jax.ShapeDtypeStruct((ND, 8, 128), jnp...]
where the time goes in v2:
time: 89.6 us; the launch traced here: 89.3 us
  Pallas kernels  56.8 us (63%)
  waiting for transfers between devices  18.8 us (21%)
  starting transfers between devices  11.5 us (13%)
  local copies, waits for them, and re-layouts  2.23 us (2%)
    pallas_call x1, Pallas kernels, z_transform(): pl.pallas_call(z_kernel, out_shape=jax.ShapeDtypeStruct((ND * ROWS, 2 * L...  27.6 us
    all_to_all x1, waiting for transfers between devices, on_device(): lax.all_to_all(msg, ('row', 'col'), split_axis=0, concat_axis=0, tiled=True)  18.8 us
    pallas_call x1, Pallas kernels, x_transform(): pl.pallas_call(x_kernel, out_shape=jax.ShapeDtypeStruct((ND, 8, 128), jnp...  14.7 us
    pallas_call x1, Pallas kernels, sum_up(): pl.pallas_call(sum_kernel, out_shape=jax.ShapeDtypeStruct((6, 128), jnp.f...  14.5 us
    all_to_all x1, starting transfers between devices, on_device(): lax.all_to_all(msg, ('row', 'col'), split_axis=0, concat_axis=0, tiled=True)  11.5 us
  transfers between devices with their start and end apart: 1, of which 1 were waited for; matrix products, arithmetic and copies ran while one was open for 0% of the time, Pallas kernels for 0%

profile of v2, /device:TPU:1, one launch (start us, length us, event | category | flops | bytes accessed | tf_op | source)
XLA Modules:
  0.0 89.3 jit_solution(9371362489095856135)
XLA Ops:
  0.0 27.6 %shard_map.73 = bf16[2048,256]{1,0:T(8,128)(2,1)} custom-call(bf16[6,40,7680]{2,1,0:T(8,128)(2,1)} %bitcast.7, bf16[4,1024,1920]{2,1,0:T(8,128)(2,1)} %constant.19.clone.tab_ref), custom_call_target="tpu_custom_call" | custom-call | tf_op jit(solution)/shard_map/pallas_call | solution.py:130
  27.6 11.5 %all-to-all-start = ((bf16[128,16,256]{2,1,0:T(8,128)(2,1)}), bf16[128,16,256]{2,1,0:T(8,128)(2,1)S(1)}, u32[]{:S(2)}, u32[]{:S(2)}) async-start(bf16[128,16,256]{2,1,0:T(8,128)(2,1)} %bitcast.5), calls=%async_computation | async-start | bytes 2097152 | tf_op jit(solution)/shard_map/all_to_all | solution.py:373
  39.1 18.8 %all-to-all-done = bf16[128,16,256]{2,1,0:T(8,128)(2,1)S(1)} async-done(((bf16[128,16,256]{2,1,0:T(8,128)(2,1)}), bf16[128,16,256]{2,1,0:T(8,128)(2,1)S(1)}, u32[]{:S(2)}, u32[]{:S(2)}) %all-to-all-start) | async-done | bytes 1048608 | tf_op jit(solution)/shard_map/all_to_all | solution.py:373
  57.9 0.0 copy-start
  57.9 1.0 %copy-done = bf16[128,16,256]{2,1,0:T(8,128)(2,1)} copy-done((bf16[128,16,256]{2,1,0:T(8,128)(2,1)}, bf16[128,16,256]{2,1,0:T(8,128)(2,1)S(1)}, u32[]{:S(2)}) %copy-start) | copy-done | bytes 1048600
  58.9 14.7 %shard_map.74.sums_ref = f32[128,8,128]{2,1,0:T(8,128)} custom-call(s32[1]{0:T(128)} %bitcast.me_ref, s32[128]{0:T(128)} %place_ref.1, bf16[2048,256]{1,0:T(8,128)(2,1)} %bitcast.6, s32[16,2048]{1,0:T(8,128)} %lab_ref.1, bf16[512,512]{1,0:T(8,128)(2,1)} %constant.20.clone.first_ref, f32[2,256,128]{2,1,0:T(8,128)} %constant.21.clone.tw_ref, ...), custom_call_target="tpu_custom_call" | custom-call | tf_op jit(solution)/shard_map/pallas_call | solution.py:251
  73.5 14.5 %shard_map.75 = f32[6,128]{1,0:T(8,128)} custom-call(f32[128,8,128]{2,1,0:T(8,128)} %shard_map.74.sums_ref), custom_call_target="tpu_custom_call" | custom-call | tf_op jit(solution)/shard_map/pallas_call | solution.py:327
  88.1 1.3 %copy.8 = f32[6,1,128]{2,1,0:T(1,128)} copy(f32[6,1,128]{2,0,1:T(8,128)} %bitcast.8) | data formatting | bytes 6144 | tf_op jit(solution)/shard_map/reshape | solution.py:377
Async XLA Ops:
  27.6 30.3 %all-to-all-start = ((bf16[128,16,256]{2,1,0:T(8,128)(2,1)}), bf16[128,16,256]{2,1,0:T(8,128)(2,1)S(1)}, u32[]{:S(2)}, u32[]{:S(2)}) async-start(bf16[128,16,256]{2,1,0:T(8,128)(2,1)} %bitcast.5), calls=%async_computation | async-start | bytes 2097152 | tf_op jit(solution)/shard_map/all_to_all | solution.py:373
  57.9 1.0 %copy-start = (bf16[128,16,256]{2,1,0:T(8,128)(2,1)}, bf16[128,16,256]{2,1,0:T(8,128)(2,1)S(1)}, u32[]{:S(2)}) copy-start(bf16[128,16,256]{2,1,0:T(8,128)(2,1)S(1)} %all-to-all-done) | copy-start | bytes 3145732

commit v3 on v2

v3 whole, which is shorter than its diff:
```python
import math

import jax
import jax.numpy as jnp
import ml_dtypes
import numpy as np
from jax import lax
from jax.experimental import pallas as pl
from jax.experimental.pallas import tpu as pltpu
from jax.sharding import PartitionSpec as P

KX = 5120
KZ = 7680
NX = 10240
ZW = 2048
XW = 2048
ND = 128
MODES = 40
QK = KZ // 4
HALF = 1024
ROWS = 16
LB = 128
NBLK = 128
LANES = 128
MESH = pl.DeviceIdType.MESH
NT = (((1,), (1,)), ((), ()))
VMEM_LIMIT = 60 * 1024 * 1024


def split(table):
    high = table.astype(ml_dtypes.bfloat16)
    low = (table - high.astype(np.float64)).astype(ml_dtypes.bfloat16)
    return high, low


def z_tables():
    za = np.arange(4)[:, None, None]
    zq = np.arange(4)[None, :, None]
    d = np.arange(ND)[None, None, :]
    z = (16 * d + 4 * zq + za).reshape(4, 512)
    cycle = (np.arange(KZ).astype(np.float32) * np.float32(2.0 * math.pi / KZ)).astype(np.float32)
    phase = (z[:, :, None] * np.arange(HALF)[None, None, :]) % KZ
    kept = np.arange(HALF) <= QK // 2
    cosine = np.where(kept, np.cos(cycle)[phase], 0.0).astype(ml_dtypes.bfloat16)
    sine = np.where(kept, np.sin(cycle)[phase], 0.0).astype(ml_dtypes.bfloat16)
    table = np.concatenate([cosine, sine], 2)
    mirror = np.zeros((2, 256, 128), np.float32)
    lane = np.arange(128)
    mirror[:, 128 - lane, lane] = 1.0
    mirror[1, :, 64] = 0.0
    return table, mirror.astype(ml_dtypes.bfloat16)


def x_tables():
    s = np.arange(ND)
    xa = np.arange(256)
    angle = 2.0 * math.pi * ((xa[:, None] * s[None, :]) % 256) / 256
    real_rows = np.concatenate([np.cos(angle), -np.sin(angle)], 1)
    imag_rows = np.concatenate([np.sin(angle), np.cos(angle)], 1)
    first = np.concatenate(split(np.concatenate([real_rows, imag_rows], 0)), 1)
    m = np.zeros(LANES, np.int64)
    m[: 3 * MODES] = np.arange(3 * MODES) % MODES
    angle = 2.0 * math.pi * (xa[:, None] * m[None, :]) / NX
    twiddle = np.stack([np.cos(angle), np.sin(angle)]).astype(np.float32)
    xb = np.arange(8)
    last = np.zeros((3, 8, 2, LANES))
    for c in range(3):
        angle = 2.0 * math.pi * ((xb[:, None] * np.arange(MODES)[None, :]) % MODES) / MODES
        last[c, :, 0, c * MODES : (c + 1) * MODES] = np.cos(angle)
        last[c, :, 1, c * MODES : (c + 1) * MODES] = -np.sin(angle)
    last = last.reshape(24, 2 * LANES)
    high, low = split(last)
    last = np.concatenate([high, low], 0)
    return first, twiddle, last


def add(p, q):
    return (p[0] + q[0], p[1] + q[1])


def sub(p, q):
    return (p[0] - q[0], p[1] - q[1])


def turn(p):
    return (-p[1], p[0])


def fill(spec, mirror_ref, coef, pair):
    pad = jnp.zeros((LANES - 3 * MODES, 128), jnp.float32)
    for block in range(8):
        turned = []
        for ka in range(4):
            start = ka * QK + (14 - block) * 128
            width = 128 if block == 0 else 256
            matrix = mirror_ref[1 if block == 7 else 0, 0:width, :]
            turned.append(jnp.dot(spec[:, start : start + width], matrix, preferred_element_type=jnp.float32))
        pieces = {}
        for c in range(3):
            near, far = [], []
            for ka in range(4):
                start = ka * QK + block * 128
                x = spec[80 * c : 80 * c + 80, start : start + 128].astype(jnp.float32)
                near.append((x[0:40], x[40:80]))
                far.append((turned[ka][80 * c : 80 * c + 40], turned[ka][80 * c + 40 : 80 * c + 80]))
            sides = []
            for x in (near, far):
                if pair == 0:
                    even, odd = add(x[0], x[2]), add(x[1], x[3])
                else:
                    even, odd = sub(x[0], x[2]), turn(sub(x[1], x[3]))
                sides.append((add(even, odd), sub(even, odd)))
            for zaa in range(2):
                y, r = sides[0][zaa], sides[1][zaa]
                if pair == 1:
                    r = turn(r)
                if zaa == 0:
                    e, o = add(y, r), sub(y, r)
                else:
                    e, o = sub(y, r), add(y, r)
                for name, value in ((0, e[0]), (1, e[1]), (2, -o[1]), (3, o[0])):
                    pieces.setdefault((zaa, name), []).append(value)
        for (zaa, name), values in pieces.items():
            whole = jnp.concatenate(values + [pad], 0)
            top = whole.astype(jnp.bfloat16)
            rows = slice(name % 2 * LANES, (name % 2 + 1) * LANES)
            cols = slice(name // 2 * HALF + block * 128, name // 2 * HALF + (block + 1) * 128)
            coef[pair, zaa, 0, rows, cols] = top
            coef[pair, zaa, 1, rows, cols] = (whole - top.astype(jnp.float32)).astype(jnp.bfloat16)


def plane(tab, coef, wide, msg, pair):
    for zaa in range(2):
        table = tab[pair + 2 * zaa]
        v = lax.dot_general(table, coef[pair, zaa, 0], NT, preferred_element_type=jnp.float32)
        v = v + lax.dot_general(table, coef[pair, zaa, 1], NT, preferred_element_type=jnp.float32)
        for zq in range(4):
            for part in range(2):
                wide[pl.ds(8 * zaa + 2 * zq + part, ND, stride=ROWS), :] = v[
                    zq * ND : (zq + 1) * ND, part * LANES : (part + 1) * LANES
                ]
    msg[pair] = wide[...].astype(jnp.bfloat16).reshape(ND, ROWS, LANES)


def enstrophy(recv, wide, mats, top, rest, first_ref, tw_ref, last_ref, enst, pair):
    scale = 2.0 / math.sqrt(2.0 * KX * KZ)
    wide[...] = recv[pair].reshape(ND * ROWS, LANES).astype(jnp.float32)
    lane = lax.broadcasted_iota(jnp.int32, (ROWS, LANES), 1)
    factor = jnp.where((lane == 0) | (lane == MODES) | (lane == 2 * MODES), 0.5, 1.0)
    wide[0:ROWS, :] = wide[0:ROWS, :] * factor
    for i in range(8):
        cols = slice(i * LANES, (i + 1) * LANES)
        for part in range(2):
            mat = wide[pl.ds(2 * i + part, ND, stride=ROWS), :].astype(jnp.bfloat16)
            mats[part * ND : (part + 1) * ND, cols] = mat
            mats[(part + 2) * ND : (part + 3) * ND, cols] = mat
    cosine, sine = tw_ref[0], tw_ref[1]
    for two in range(4):
        both = mats[:, two * 256 : (two + 1) * 256]
        y = jnp.dot(first_ref[...], both, preferred_element_type=jnp.float32)
        for half in range(2):
            yr = y[0:256, half * LANES : (half + 1) * LANES]
            yi = y[256:512, half * LANES : (half + 1) * LANES]
            t = jnp.concatenate([yr * cosine - yi * sine, yr * sine + yi * cosine], 1)
            high = t.astype(jnp.bfloat16)
            rows = slice((two * 2 + half) * 256, (two * 2 + half + 1) * 256)
            top[rows, :] = high
            rest[rows, :] = (t - high.astype(jnp.float32)).astype(jnp.bfloat16)
    v = lax.dot_general(last_ref[...], top[...], NT, preferred_element_type=jnp.float32)
    v = v[0:24] + v[24:48]
    v = v + lax.dot_general(last_ref[0:24], rest[...], NT, preferred_element_type=jnp.float32)
    v = v * scale
    enst[...] = v[0:8] * v[0:8] + v[8:16] * v[8:16] + v[16:24] * v[16:24]


def zpoint(pair, i):
    return 4 * (i % 4) + 2 * (i // 4) + pair


def spread(row, count):
    tile = jnp.broadcast_to(row, (16, row.shape[1])).astype(jnp.bfloat16)
    return jnp.concatenate([tile] * (count // 16), 0)


def label_sums(me, targets, enst, acc0, acc1, lhs_a, rhs_a, lhs_b, rhs_b, pair):
    upos = (
        lax.broadcasted_iota(jnp.int32, (8, 256), 0) * 256 + lax.broadcasted_iota(jnp.int32, (8, 256), 1)
    ).astype(jnp.float32) / XW - 0.5
    row64 = lax.broadcasted_iota(jnp.int32, (64, 256), 0).astype(jnp.float32).astype(jnp.bfloat16)
    row256 = lax.broadcasted_iota(jnp.int32, (256, 256), 0).astype(jnp.float32).astype(jnp.bfloat16)
    one = jnp.ones((), jnp.bfloat16)
    zero = jnp.zeros((), jnp.bfloat16)

    def build(i, lhs, rhs):
        z = zpoint(pair, i)
        e = enst[:, i * 256 : (i + 1) * 256]
        ehigh = e.astype(jnp.bfloat16).astype(jnp.float32)
        eu = e * upos
        values = [ehigh, e - ehigh, eu, eu * upos]
        for xb in range(8):
            cols = slice(xb * 256, (xb + 1) * 256)
            lab = targets[z : z + 1, cols]
            hit = spread((lab >> 8).astype(jnp.float32), 64) == row64
            lhs[0:64, cols] = jnp.where(hit, one, zero)
            for j, value in enumerate(values):
                lhs[(j + 1) * 64 : (j + 2) * 64, cols] = jnp.where(hit, spread(value[xb : xb + 1], 64), zero)
            near = spread((lab & 255).astype(jnp.float32), 256) == row256
            rhs[:, cols] = jnp.where(near, one, zero)

    def collect(i, lhs, rhs):
        t = lax.dot_general(lhs[...], rhs[...], NT, preferred_element_type=jnp.float32)
        w = (me * ROWS + zpoint(pair, i)).astype(jnp.float32) / ZW - 0.5
        e_sum = t[64:128] + t[128:192]
        eu_sum = t[192:256]
        terms = [t[0:64], e_sum, eu_sum, e_sum * w, t[256:320], eu_sum * w, e_sum * (w * w)]
        for j, term in enumerate(terms):
            acc0[j * 64 : (j + 1) * 64, :] += term[:, :128]
            acc1[j * 64 : (j + 1) * 64, :] += term[:, 128:]

    buffers = ((lhs_a, rhs_a), (lhs_b, rhs_b))
    build(0, *buffers[0])
    for i in range(8):
        if i < 7:
            build(i + 1, *buffers[(i + 1) % 2])
        collect(i, *buffers[i % 2])


def owner_of(core, q):
    return (q // 16 * 2 + core, q % 16)


def kernel(
    spec_hbm, tab_hbm, lab_ref, place_ref, mirror_ref, first_ref, tw_ref, last_ref, out_ref,
    spec, tab, coef, wide, msg, recv, targets, mats, top, rest, enst, acc0, acc1,
    lhs_a, rhs_a, lhs_b, rhs_b, table, mate, part, parts,
    spec_sem, tab_sem, own_sem, plane_send, plane_recv, pair_send, pair_recv, sum_send, sum_recv,
):
    row = lax.axis_index("row")
    col = lax.axis_index("col")
    me = row * 16 + col
    core = row % 2
    mine = row // 2 * 16 + col
    load = pltpu.make_async_copy(spec_hbm, spec, spec_sem)
    load.start()
    order = (0, 2, 1, 3)
    loads = [pltpu.make_async_copy(tab_hbm.at[za], tab.at[za], tab_sem.at[za]) for za in range(4)]
    for za in order:
        loads[za].start()
    barrier = pltpu.get_barrier_semaphore()

    def greet(j, carry):
        d = lax.rem(me + j, ND)
        pl.semaphore_signal(barrier, inc=1, device_id=(d // 16, d % 16), device_id_type=MESH)
        return carry

    lax.fori_loop(1, ND, greet, 0)

    places = jnp.broadcast_to(place_ref[...], (16, LB))
    for i in range(XW // LB):
        cols = slice(i * LB, (i + 1) * LB)
        lab = lab_ref[:, cols]
        targets[:, cols] = jnp.take_along_axis(places, lab >> 7, axis=1) * LB + (lab & 127)
    acc0[...] = jnp.zeros_like(acc0)
    acc1[...] = jnp.zeros_like(acc1)

    load.wait()
    owns = []
    for pair in range(2):
        fill(spec, mirror_ref, coef, pair)
        for zaa in range(2):
            loads[pair + 2 * zaa].wait()
        plane(tab, coef, wide, msg, pair)
        if pair == 0:
            pl.semaphore_wait(barrier, ND - 1)

        def send(j, carry, pair=pair):
            d = lax.rem(me + j, ND)
            pltpu.make_async_remote_copy(
                src_ref=msg.at[pair, d],
                dst_ref=recv.at[pair, me],
                send_sem=plane_send.at[pair],
                recv_sem=plane_recv.at[pair],
                device_id=(d // 16, d % 16),
                device_id_type=MESH,
            ).start()
            return carry

        lax.fori_loop(1, ND, send, 0)
        own = pltpu.make_async_copy(msg.at[pair, me], recv.at[pair, me], own_sem.at[pair])
        own.start()
        owns.append(own)

    for pair in range(2):
        owns[pair].wait()
        others = recv.at[pair, pl.ds(0, ND - 1)]
        pltpu.make_async_copy(others, others, plane_recv.at[pair]).wait()
        enstrophy(recv, wide, mats, top, rest, first_ref, tw_ref, last_ref, enst, pair)
        label_sums(me, targets, enst, acc0, acc1, lhs_a, rhs_a, lhs_b, rhs_b, pair)

    for place in range(NBLK):
        table[place % 2, place % 8 // 2 * 16 + place // 8] = (acc0, acc1)[place % 2][
            pl.ds(place // 2, 8, stride=64), :
        ]
    swap = pltpu.make_async_remote_copy(
        src_ref=table.at[1 - core],
        dst_ref=mate,
        send_sem=pair_send,
        recv_sem=pair_recv,
        device_id=(row + 1 - 2 * core, col),
        device_id_type=MESH,
    )
    swap.start()
    swap.wait()
    part[...] = table[core] + mate[...]

    def send_sum(j, carry):
        q = lax.rem(mine + j, 64)
        pltpu.make_async_remote_copy(
            src_ref=part.at[q],
            dst_ref=parts.at[mine],
            send_sem=sum_send,
            recv_sem=sum_recv,
            device_id=owner_of(core, q),
            device_id_type=MESH,
        ).start()
        return carry

    lax.fori_loop(1, 64, send_sum, 0)
    parts[mine] = part[mine]
    every = parts.at[pl.ds(0, 63)]
    pltpu.make_async_copy(every, every, sum_send).wait()
    pltpu.make_async_copy(every, every, sum_recv).wait()
    for pair in range(2):
        others = msg.at[pair, pl.ds(0, ND - 1)]
        pltpu.make_async_copy(others, others, plane_send.at[pair]).wait()
    out_ref[...] = finish(jnp.sum(parts[...], 0))


def run(spec, table, labels, place, mirror, first, twiddle, last):
    vmem = pl.BlockSpec(memory_space=pltpu.VMEM)
    hbm = pl.BlockSpec(memory_space=pl.ANY)
    f32, bf16 = jnp.float32, jnp.bfloat16
    dma = pltpu.SemaphoreType.DMA
    return pl.pallas_call(
        kernel,
        out_shape=jax.ShapeDtypeStruct((6, 128), f32),
        in_specs=[hbm, hbm] + [vmem] * 6,
        out_specs=vmem,
        scratch_shapes=[
            pltpu.VMEM((6 * MODES, KZ), bf16),
            pltpu.VMEM((4, 512, 2 * HALF), bf16),
            pltpu.VMEM((2, 2, 2, 2 * LANES, 2 * HALF), bf16),
            pltpu.VMEM((ND * ROWS, LANES), f32),
            pltpu.VMEM((2, ND, ROWS, LANES), bf16),
            pltpu.VMEM((2, ND, ROWS, LANES), bf16),
            pltpu.VMEM((ROWS, XW), jnp.int32),
            pltpu.VMEM((512, 8 * LANES), bf16),
            pltpu.VMEM((8 * 256, 2 * LANES), bf16),
            pltpu.VMEM((8 * 256, 2 * LANES), bf16),
            pltpu.VMEM((8, 8 * 256), f32),
            pltpu.VMEM((512, 128), f32),
            pltpu.VMEM((512, 128), f32),
            pltpu.VMEM((320, XW), bf16),
            pltpu.VMEM((256, XW), bf16),
            pltpu.VMEM((320, XW), bf16),
            pltpu.VMEM((256, XW), bf16),
            pltpu.VMEM((2, 64, 8, 128), f32),
            pltpu.VMEM((64, 8, 128), f32),
            pltpu.VMEM((64, 8, 128), f32),
            pltpu.VMEM((64, 8, 128), f32),
            dma, dma((4,)), dma((2,)), dma((2,)), dma((2,)), dma, dma, dma, dma,
        ],
        compiler_params=pltpu.CompilerParams(
            collective_id=0, has_side_effects=True, vmem_limit_bytes=VMEM_LIMIT
        ),
    )(spec, table, labels, place, mirror, first, twiddle, last)


def finish(centred):
    count, s1, u1, w1, uu, uw, ww = (centred[j] for j in range(7))
    s2 = u1 + 0.5 * s1
    s3 = w1 + 0.5 * s1
    s4 = uu + u1 + 0.25 * s1
    s5 = uw + 0.5 * (u1 + w1) + 0.25 * s1
    s6 = ww + w1 + 0.25 * s1
    weight = jnp.maximum(s1, 1.0)
    centre_x = s2 / weight
    centre_z = s3 / weight
    return jnp.stack(
        [
            s1 / jnp.maximum(count, 1.0),
            centre_x,
            centre_z,
            12.0 * (s4 / weight - centre_x * centre_x),
            12.0 * (s5 / weight - centre_x * centre_z),
            12.0 * (s6 / weight - centre_z * centre_z),
        ],
        0,
    )


def solution(mesh):
    table, mirror = z_tables()
    first, twiddle, last = x_tables()

    def on_device(spectral, labels, block_place):
        spec = spectral.reshape(6 * MODES, KZ)
        out = run(spec, table, labels, block_place.reshape(1, NBLK), mirror, first, twiddle, last)
        return out.reshape(6, 1, 128)

    in_specs = (P(None, None, ("row", "col"), None), P(("row", "col"), None), P())
    return jax.shard_map(on_device, mesh=mesh, in_specs=in_specs, out_specs=P(None, "col", "row"), check_vma=False)
```

time: 89.6 us -> 53.8 us (0.60)
  waiting for transfers between devices: 18.8 us -> 0 us
  starting transfers between devices: 11.5 us -> 0 us
  Pallas kernels: 56.8 us -> 52.4 us
  local copies, waits for them, and re-layouts: 2.23 us -> 1.26 us
    all_to_all x1 -> x0, waiting for transfers between devices: 18.8 us -> none  [on_device(): lax.all_to_all(msg, ('row', 'col'), split_axis=0, concat_axis=0, tiled=True)]
    all_to_all x1 -> x0, starting transfers between devices: 11.5 us -> none  [on_device(): lax.all_to_all(msg, ('row', 'col'), split_axis=0, concat_axis=0, tiled=True)]
    pallas_call x3 -> x1, Pallas kernels: 56.8 us -> 52.4 us  [run(): pl.pallas_call(kernel, out_shape=jax.ShapeDtypeStruct((6, 128), f32), in_...]
    unnamed x2 -> x0, local copies, waits for them, and re-layouts: 0.97 us -> none
  transfers between devices with their start and end apart: 1 -> 0, of which waited for: 1 -> 0; matrix products, arithmetic and copies ran while one was open for 0% -> 0% of each run, Pallas kernels for 0% -> 0%
where the time goes in v3:
time: 53.8 us; the launch traced here: 53.7 us
  Pallas kernels  52.4 us (97%)
  local copies, waits for them, and re-layouts  1.26 us (2%)
    pallas_call x1, Pallas kernels, run(): pl.pallas_call(kernel, out_shape=jax.ShapeDtypeStruct((6, 128), f32), in_...  52.4 us
    reshape x1, local copies, waits for them, and re-layouts, on_device(): return out.reshape(6, 1, 128)  1.26 us

profile of v3, /device:TPU:1, one launch (start us, length us, event | category | flops | bytes accessed | tf_op | source)
XLA Modules:
  0.0 53.7 jit_solution(6076284121804366961)
XLA Ops:
  0.0 52.4 %shard_map.82 = f32[6,128]{1,0:T(8,128)} custom-call(bf16[240,7680]{1,0:T(8,128)(2,1)} %bitcast.3, bf16[4,512,2048]{2,1,0:T(8,128)(2,1)} %constant.10.clone.tab_hbm, s32[16,2048]{1,0:T(8,128)} %lab_ref.1, s32[1,128]{1,0:T(1,128)} %bitcast.5, bf16[2,256,128]{2,1,0:T(8,128)(2,1)} %constant.11.clone.mirror_ref, bf16[512,512]{1,0:T(8,128)(2,1)} %constant.12.clone.first_ref, ...), custom_call_target="tpu_custom_call" | custom-call | tf_op jit(solution)/shard_map/pallas_call | solution.py:344
  52.4 1.3 %copy.9 = f32[6,1,128]{2,1,0:T(1,128)} copy(f32[6,1,128]{2,0,1:T(8,128)} %bitcast.4) | data formatting | bytes 6144 | tf_op jit(solution)/shard_map/reshape | solution.py:409

commit v4 on v3

--- a/solution.py
+++ b/solution.py
@@ -193,13 +193,13 @@
 
     def build(i, lhs, rhs):
         z = zpoint(pair, i)
-        e = enst[:, i * 256 : (i + 1) * 256]
+        e = enst[:, pl.ds(pl.multiple_of(i * 256, 256), 256)]
         ehigh = e.astype(jnp.bfloat16).astype(jnp.float32)
         eu = e * upos
         values = [ehigh, e - ehigh, eu, eu * upos]
         for xb in range(8):
             cols = slice(xb * 256, (xb + 1) * 256)
-            lab = targets[z : z + 1, cols]
+            lab = targets[pl.ds(z, 1), cols]
             hit = spread((lab >> 8).astype(jnp.float32), 64) == row64
             lhs[0:64, cols] = jnp.where(hit, one, zero)
             for j, value in enumerate(values):
@@ -217,12 +217,16 @@
             acc0[j * 64 : (j + 1) * 64, :] += term[:, :128]
             acc1[j * 64 : (j + 1) * 64, :] += term[:, 128:]
 
-    buffers = ((lhs_a, rhs_a), (lhs_b, rhs_b))
-    build(0, *buffers[0])
-    for i in range(8):
-        if i < 7:
-            build(i + 1, *buffers[(i + 1) % 2])
-        collect(i, *buffers[i % 2])
+    build(0, lhs_a, rhs_a)
+
+    def two_rows(n, carry):
+        build(2 * n + 1, lhs_b, rhs_b)
+        collect(2 * n, lhs_a, rhs_a)
+        build(lax.rem(2 * n + 2, 8), lhs_a, rhs_a)
+        collect(2 * n + 1, lhs_b, rhs_b)
+        return carry
+
+    lax.fori_loop(0, 4, two_rows, 0)
 
 
 def owner_of(core, q):
@@ -244,8 +248,6 @@
     load.start()
     order = (0, 2, 1, 3)
     loads = [pltpu.make_async_copy(tab_hbm.at[za], tab.at[za], tab_sem.at[za]) for za in range(4)]
-    for za in order:
-        loads[za].start()
     barrier = pltpu.get_barrier_semaphore()
 
     def greet(j, carry):
@@ -264,6 +266,8 @@
     acc1[...] = jnp.zeros_like(acc1)
 
     load.wait()
+    for za in order:
+        loads[za].start()
     owns = []
     for pair in range(2):
         fill(spec, mirror_ref, coef, pair)

time: 53.8 us -> 46.5 us (0.86)
  Pallas kernels: 52.4 us -> 45.1 us
    pallas_call x1, Pallas kernels: 52.4 us -> 45.1 us  [run(): pl.pallas_call(kernel, out_shape=jax.ShapeDtypeStruct((6, 128), f32), in_...]
where the time goes in v4:
time: 46.5 us; the launch traced here: 46.3 us
  Pallas kernels  45.1 us (97%)
  local copies, waits for them, and re-layouts  1.26 us (3%)
    pallas_call x1, Pallas kernels, run(): pl.pallas_call(kernel, out_shape=jax.ShapeDtypeStruct((6, 128), f32), in_...  45.1 us
    reshape x1, local copies, waits for them, and re-layouts, on_device(): return out.reshape(6, 1, 128)  1.26 us

profile of v4, /device:TPU:1, one launch (start us, length us, event | category | flops | bytes accessed | tf_op | source)
XLA Modules:
  0.0 46.3 jit_solution(11682015205492856761)
XLA Ops:
  0.0 45.1 %shard_map.82 = f32[6,128]{1,0:T(8,128)} custom-call(bf16[240,7680]{1,0:T(8,128)(2,1)} %bitcast.3, bf16[4,512,2048]{2,1,0:T(8,128)(2,1)} %constant.10.clone.tab_hbm, s32[16,2048]{1,0:T(8,128)} %lab_ref.1, s32[1,128]{1,0:T(1,128)} %bitcast.5, bf16[2,256,128]{2,1,0:T(8,128)(2,1)} %constant.11.clone.mirror_ref, bf16[512,512]{1,0:T(8,128)(2,1)} %constant.12.clone.first_ref, ...), custom_call_target="tpu_custom_call" | custom-call | tf_op jit(solution)/shard_map/pallas_call | solution.py:348
  45.1 1.3 %copy.9 = f32[6,1,128]{2,1,0:T(1,128)} copy(f32[6,1,128]{2,0,1:T(8,128)} %bitcast.4) | data formatting | bytes 6144 | tf_op jit(solution)/shard_map/reshape | solution.py:413

commit v5 on v4

--- a/solution.py
+++ b/solution.py
@@ -217,16 +217,16 @@
             acc0[j * 64 : (j + 1) * 64, :] += term[:, :128]
             acc1[j * 64 : (j + 1) * 64, :] += term[:, 128:]
 
+    buffers = ((lhs_a, rhs_a), (lhs_b, rhs_b))
     build(0, lhs_a, rhs_a)
 
-    def two_rows(n, carry):
-        build(2 * n + 1, lhs_b, rhs_b)
-        collect(2 * n, lhs_a, rhs_a)
-        build(lax.rem(2 * n + 2, 8), lhs_a, rhs_a)
-        collect(2 * n + 1, lhs_b, rhs_b)
+    def four_rows(n, carry):
+        for k in range(4):
+            build(4 * n + k + 1 if k < 3 else lax.rem(4 * n + 4, 8), *buffers[(k + 1) % 2])
+            collect(4 * n + k, *buffers[k % 2])
         return carry
 
-    lax.fori_loop(0, 4, two_rows, 0)
+    lax.fori_loop(0, 2, four_rows, 0)
 
 
 def owner_of(core, q):
@@ -347,7 +347,7 @@
     dma = pltpu.SemaphoreType.DMA
     return pl.pallas_call(
         kernel,
-        out_shape=jax.ShapeDtypeStruct((6, 128), f32),
+        out_shape=pltpu.VMEM((6, 128), f32),
         in_specs=[hbm, hbm] + [vmem] * 6,
         out_specs=vmem,
         scratch_shapes=[

time: 46.5 us -> 44.7 us (0.961)
  Pallas kernels: 45.1 us -> 44 us
  local copies, waits for them, and re-layouts: 1.26 us -> 0.58 us
    pallas_call x1, Pallas kernels: 45.1 us -> 44 us  [run(): pl.pallas_call(kernel, out_shape=pltpu.VMEM((6, 128), f32), in_specs=[hbm...]
    reshape x1, local copies, waits for them, and re-layouts: 1.26 us -> 0.58 us  [on_device(): return out.reshape(6, 1, 128)]
where the time goes in v5:
time: 44.7 us; the launch traced here: 44.6 us
  Pallas kernels  44 us (98%)
  local copies, waits for them, and re-layouts  0.58 us (1%)
    pallas_call x1, Pallas kernels, run(): pl.pallas_call(kernel, out_shape=pltpu.VMEM((6, 128), f32), in_specs=[hbm...  44 us

profile of v5, /device:TPU:1, one launch (start us, length us, event | category | flops | bytes accessed | tf_op | source)
XLA Modules:
  0.0 44.6 jit_solution(10716845886951715231)
XLA Ops:
  0.0 44.0 %shard_map.82 = f32[6,128]{1,0:T(8,128)S(1)} custom-call(bf16[240,7680]{1,0:T(8,128)(2,1)} %bitcast.4, bf16[4,512,2048]{2,1,0:T(8,128)(2,1)} %constant.10.clone.tab_hbm, s32[16,2048]{1,0:T(8,128)} %lab_ref.1, s32[1,128]{1,0:T(1,128)} %bitcast.5, bf16[2,256,128]{2,1,0:T(8,128)(2,1)} %constant.11.clone.mirror_ref, bf16[512,512]{1,0:T(8,128)(2,1)} %constant.12.clone.first_ref, ...), custom_call_target="tpu_custom_call" | custom-call | tf_op jit(solution)/shard_map/pallas_call | solution.py:348
  44.0 0.6 %copy.9 = f32[6,1,128]{2,1,0:T(1,128)} copy(f32[6,1,128]{2,0,1:T(8,128)S(1)} %bitcast.3) | data formatting | bytes 6144 | tf_op jit(solution)/shard_map/reshape | solution.py:413

commit v6 on v5

--- a/solution.py
+++ b/solution.py
@@ -122,18 +122,15 @@
                     pieces.setdefault((zaa, name), []).append(value)
         for (zaa, name), values in pieces.items():
             whole = jnp.concatenate(values + [pad], 0)
-            top = whole.astype(jnp.bfloat16)
             rows = slice(name % 2 * LANES, (name % 2 + 1) * LANES)
             cols = slice(name // 2 * HALF + block * 128, name // 2 * HALF + (block + 1) * 128)
-            coef[pair, zaa, 0, rows, cols] = top
-            coef[pair, zaa, 1, rows, cols] = (whole - top.astype(jnp.float32)).astype(jnp.bfloat16)
+            coef[pair, zaa, rows, cols] = whole.astype(jnp.bfloat16)
 
 
 def plane(tab, coef, wide, msg, pair):
     for zaa in range(2):
         table = tab[pair + 2 * zaa]
-        v = lax.dot_general(table, coef[pair, zaa, 0], NT, preferred_element_type=jnp.float32)
-        v = v + lax.dot_general(table, coef[pair, zaa, 1], NT, preferred_element_type=jnp.float32)
+        v = lax.dot_general(table, coef[pair, zaa], NT, preferred_element_type=jnp.float32)
         for zq in range(4):
             for part in range(2):
                 wide[pl.ds(8 * zaa + 2 * zq + part, ND, stride=ROWS), :] = v[
@@ -235,7 +232,7 @@
 
 def kernel(
     spec_hbm, tab_hbm, lab_ref, place_ref, mirror_ref, first_ref, tw_ref, last_ref, out_ref,
-    spec, tab, coef, wide, msg, recv, targets, mats, top, rest, enst, acc0, acc1,
+    spec, tab, coef, wide, msg, recv, targets, mats, top, rest, enst, acc,
     lhs_a, rhs_a, lhs_b, rhs_b, table, mate, part, parts,
     spec_sem, tab_sem, own_sem, plane_send, plane_recv, pair_send, pair_recv, sum_send, sum_recv,
 ):
@@ -262,8 +259,7 @@
         cols = slice(i * LB, (i + 1) * LB)
         lab = lab_ref[:, cols]
         targets[:, cols] = jnp.take_along_axis(places, lab >> 7, axis=1) * LB + (lab & 127)
-    acc0[...] = jnp.zeros_like(acc0)
-    acc1[...] = jnp.zeros_like(acc1)
+    acc[...] = jnp.zeros_like(acc)
 
     load.wait()
     for za in order:
@@ -299,12 +295,13 @@
         others = recv.at[pair, pl.ds(0, ND - 1)]
         pltpu.make_async_copy(others, others, plane_recv.at[pair]).wait()
         enstrophy(recv, wide, mats, top, rest, first_ref, tw_ref, last_ref, enst, pair)
-        label_sums(me, targets, enst, acc0, acc1, lhs_a, rhs_a, lhs_b, rhs_b, pair)
-
-    for place in range(NBLK):
-        table[place % 2, place % 8 // 2 * 16 + place // 8] = (acc0, acc1)[place % 2][
-            pl.ds(place // 2, 8, stride=64), :
-        ]
+        label_sums(me, targets, enst, acc.at[0], acc.at[1], lhs_a, rhs_a, lhs_b, rhs_b, pair)
+
+    def hand_out(half):
+        for n in range(64):
+            table[half, n % 4 * 16 + n // 4] = acc[half, pl.ds(n, 8, stride=64), :]
+
+    hand_out(1 - core)
     swap = pltpu.make_async_remote_copy(
         src_ref=table.at[1 - core],
         dst_ref=mate,
@@ -314,6 +311,7 @@
         device_id_type=MESH,
     )
     swap.start()
+    hand_out(core)
     swap.wait()
     part[...] = table[core] + mate[...]
 
@@ -353,7 +351,7 @@
         scratch_shapes=[
             pltpu.VMEM((6 * MODES, KZ), bf16),
             pltpu.VMEM((4, 512, 2 * HALF), bf16),
-            pltpu.VMEM((2, 2, 2, 2 * LANES, 2 * HALF), bf16),
+            pltpu.VMEM((2, 2, 2 * LANES, 2 * HALF), bf16),
             pltpu.VMEM((ND * ROWS, LANES), f32),
             pltpu.VMEM((2, ND, ROWS, LANES), bf16),
             pltpu.VMEM((2, ND, ROWS, LANES), bf16),
@@ -362,8 +360,7 @@
             pltpu.VMEM((8 * 256, 2 * LANES), bf16),
             pltpu.VMEM((8 * 256, 2 * LANES), bf16),
             pltpu.VMEM((8, 8 * 256), f32),
-            pltpu.VMEM((512, 128), f32),
-            pltpu.VMEM((512, 128), f32),
+            pltpu.VMEM((2, 512, 128), f32),
             pltpu.VMEM((320, XW), bf16),
             pltpu.VMEM((256, XW), bf16),
             pltpu.VMEM((320, XW), bf16),

time: 44.7 us -> 42 us (0.940)
  Pallas kernels: 44 us -> 41.3 us
    pallas_call x1, Pallas kernels: 44 us -> 41.3 us  [run(): pl.pallas_call(kernel, out_shape=pltpu.VMEM((6, 128), f32), in_specs=[hbm...]
where the time goes in v6:
time: 42 us; the launch traced here: 41.9 us
  Pallas kernels  41.3 us (98%)
  local copies, waits for them, and re-layouts  0.58 us (1%)
    pallas_call x1, Pallas kernels, run(): pl.pallas_call(kernel, out_shape=pltpu.VMEM((6, 128), f32), in_specs=[hbm...  41.3 us

profile of v6, /device:TPU:1, one launch (start us, length us, event | category | flops | bytes accessed | tf_op | source)
XLA Modules:
  0.0 41.9 jit_solution(15936458188978444813)
XLA Ops:
  0.0 41.3 %shard_map.82 = f32[6,128]{1,0:T(8,128)S(1)} custom-call(bf16[240,7680]{1,0:T(8,128)(2,1)} %bitcast.4, bf16[4,512,2048]{2,1,0:T(8,128)(2,1)} %constant.10.clone.tab_hbm, s32[16,2048]{1,0:T(8,128)} %lab_ref.1, s32[1,128]{1,0:T(1,128)} %bitcast.5, bf16[2,256,128]{2,1,0:T(8,128)(2,1)} %constant.11.clone.mirror_ref, bf16[512,512]{1,0:T(8,128)(2,1)} %constant.12.clone.first_ref, ...), custom_call_target="tpu_custom_call" | custom-call | tf_op jit(solution)/shard_map/pallas_call | solution.py:346
  41.3 0.6 %copy.9 = f32[6,1,128]{2,1,0:T(1,128)} copy(f32[6,1,128]{2,0,1:T(8,128)S(1)} %bitcast.3) | data formatting | bytes 6144 | tf_op jit(solution)/shard_map/reshape | solution.py:410

commit v7 on v6

--- a/solution.py
+++ b/solution.py
@@ -226,10 +226,6 @@
     lax.fori_loop(0, 2, four_rows, 0)
 
 
-def owner_of(core, q):
-    return (q // 16 * 2 + core, q % 16)
-
-
 def kernel(
     spec_hbm, tab_hbm, lab_ref, place_ref, mirror_ref, first_ref, tw_ref, last_ref, out_ref,
     spec, tab, coef, wide, msg, recv, targets, mats, top, rest, enst, acc,
@@ -297,37 +293,44 @@
         enstrophy(recv, wide, mats, top, rest, first_ref, tw_ref, last_ref, enst, pair)
         label_sums(me, targets, enst, acc.at[0], acc.at[1], lhs_a, rhs_a, lhs_b, rhs_b, pair)
 
-    def hand_out(half):
-        for n in range(64):
-            table[half, n % 4 * 16 + n // 4] = acc[half, pl.ds(n, 8, stride=64), :]
-
-    hand_out(1 - core)
-    swap = pltpu.make_async_remote_copy(
-        src_ref=table.at[1 - core],
-        dst_ref=mate,
-        send_sem=pair_send,
-        recv_sem=pair_recv,
-        device_id=(row + 1 - 2 * core, col),
-        device_id_type=MESH,
-    )
-    swap.start()
-    hand_out(core)
-    swap.wait()
-    part[...] = table[core] + mate[...]
-
-    def send_sum(j, carry):
-        q = lax.rem(mine + j, 64)
-        pltpu.make_async_remote_copy(
-            src_ref=part.at[q],
-            dst_ref=parts.at[mine],
-            send_sem=sum_send,
-            recv_sem=sum_recv,
-            device_id=owner_of(core, q),
+    def hand_out(half, there):
+        for m in range(16):
+            table[half, there * 16 + m] = acc[half, pl.ds(there + 4 * m, 8, stride=64), :]
+
+    theres = [lax.rem(row // 2 + k, 4) for k in (2, 1, 3, 0)]
+    swaps = []
+    for k, there in enumerate(theres):
+        hand_out(1 - core, there)
+        blocks = pl.ds(there * 16, 16)
+        swap = pltpu.make_async_remote_copy(
+            src_ref=table.at[1 - core, blocks],
+            dst_ref=mate.at[blocks],
+            send_sem=pair_send.at[k],
+            recv_sem=pair_recv.at[k],
+            device_id=(row + 1 - 2 * core, col),
             device_id_type=MESH,
-        ).start()
-        return carry
-
-    lax.fori_loop(1, 64, send_sum, 0)
+        )
+        swap.start()
+        swaps.append(swap)
+    for k, there in enumerate(theres):
+        hand_out(core, there)
+        swaps[k].wait()
+        blocks = pl.ds(there * 16, 16)
+        part[blocks] = table[core, blocks] + mate[blocks]
+
+        def send_sum(j, carry, there=there):
+            c = lax.rem(col + j, 16)
+            pltpu.make_async_remote_copy(
+                src_ref=part.at[there * 16 + c],
+                dst_ref=parts.at[mine],
+                send_sem=sum_send,
+                recv_sem=sum_recv,
+                device_id=(there * 2 + core, c),
+                device_id_type=MESH,
+            ).start()
+            return carry
+
+        lax.fori_loop(1 if k == 3 else 0, 16, send_sum, 0)
     parts[mine] = part[mine]
     every = parts.at[pl.ds(0, 63)]
     pltpu.make_async_copy(every, every, sum_send).wait()
@@ -369,7 +372,7 @@
             pltpu.VMEM((64, 8, 128), f32),
             pltpu.VMEM((64, 8, 128), f32),
             pltpu.VMEM((64, 8, 128), f32),
-            dma, dma((4,)), dma((2,)), dma((2,)), dma((2,)), dma, dma, dma, dma,
+            dma, dma((4,)), dma((2,)), dma((2,)), dma((2,)), dma((4,)), dma((4,)), dma, dma,
         ],
         compiler_params=pltpu.CompilerParams(
             collective_id=0, has_side_effects=True, vmem_limit_bytes=VMEM_LIMIT

time: 42 us -> 41.7 us (level)
  no operation moved by 1% of the time
where the time goes in v7:
time: 41.7 us; the launch traced here: 41.5 us
  Pallas kernels  41 us (98%)
  local copies, waits for them, and re-layouts  0.58 us (1%)
    pallas_call x1, Pallas kernels, run(): pl.pallas_call(kernel, out_shape=pltpu.VMEM((6, 128), f32), in_specs=[hbm...  41 us

profile of v7, /device:TPU:1, one launch (start us, length us, event | category | flops | bytes accessed | tf_op | source)
XLA Modules:
  0.0 41.5 jit_solution(8372776487262233605)
XLA Ops:
  0.0 41.0 %shard_map.82 = f32[6,128]{1,0:T(8,128)S(1)} custom-call(bf16[240,7680]{1,0:T(8,128)(2,1)} %bitcast.4, bf16[4,512,2048]{2,1,0:T(8,128)(2,1)} %constant.10.clone.tab_hbm, s32[16,2048]{1,0:T(8,128)} %lab_ref.1, s32[1,128]{1,0:T(1,128)} %bitcast.5, bf16[2,256,128]{2,1,0:T(8,128)(2,1)} %constant.11.clone.mirror_ref, bf16[512,512]{1,0:T(8,128)(2,1)} %constant.12.clone.first_ref, ...), custom_call_target="tpu_custom_call" | custom-call | tf_op jit(solution)/shard_map/pallas_call | solution.py:349
  41.0 0.6 %copy.9 = f32[6,1,128]{2,1,0:T(1,128)} copy(f32[6,1,128]{2,0,1:T(8,128)S(1)} %bitcast.3) | data formatting | bytes 6144 | tf_op jit(solution)/shard_map/reshape | solution.py:413

commit v8 on v7

--- a/solution.py
+++ b/solution.py
@@ -227,7 +227,8 @@
 
 
 def kernel(
-    spec_hbm, tab_hbm, lab_ref, place_ref, mirror_ref, first_ref, tw_ref, last_ref, out_ref,
+    spec_hbm, tab_hbm, lab_hbm, place_hbm, mirror_hbm, first_hbm, tw_hbm, last_hbm, out_ref,
+    lab_ref, place_ref, mirror_ref, first_ref, tw_ref, last_ref, small_sem,
     spec, tab, coef, wide, msg, recv, targets, mats, top, rest, enst, acc,
     lhs_a, rhs_a, lhs_b, rhs_b, table, mate, part, parts,
     spec_sem, tab_sem, own_sem, plane_send, plane_recv, pair_send, pair_recv, sum_send, sum_recv,
@@ -238,6 +239,21 @@
     core = row % 2
     mine = row // 2 * 16 + col
     load = pltpu.make_async_copy(spec_hbm, spec, spec_sem)
+    smalls = [
+        pltpu.make_async_copy(source, target, small_sem.at[n])
+        for n, (source, target) in enumerate(
+            (
+                (mirror_hbm, mirror_ref),
+                (lab_hbm, lab_ref),
+                (place_hbm, place_ref),
+                (first_hbm, first_ref),
+                (tw_hbm, tw_ref),
+                (last_hbm, last_ref),
+            )
+        )
+    ]
+    for small in smalls[:3]:
+        small.start()
     load.start()
     order = (0, 2, 1, 3)
     loads = [pltpu.make_async_copy(tab_hbm.at[za], tab.at[za], tab_sem.at[za]) for za in range(4)]
@@ -250,6 +266,8 @@
 
     lax.fori_loop(1, ND, greet, 0)
 
+    for small in smalls[:3]:
+        small.wait()
     places = jnp.broadcast_to(place_ref[...], (16, LB))
     for i in range(XW // LB):
         cols = slice(i * LB, (i + 1) * LB)
@@ -260,6 +278,8 @@
     load.wait()
     for za in order:
         loads[za].start()
+    for small in smalls[3:]:
+        small.start()
     owns = []
     for pair in range(2):
         fill(spec, mirror_ref, coef, pair)
@@ -285,6 +305,8 @@
         own = pltpu.make_async_copy(msg.at[pair, me], recv.at[pair, me], own_sem.at[pair])
         own.start()
         owns.append(own)
+    for small in smalls[3:]:
+        small.wait()
 
     for pair in range(2):
         owns[pair].wait()
@@ -349,9 +371,16 @@
     return pl.pallas_call(
         kernel,
         out_shape=pltpu.VMEM((6, 128), f32),
-        in_specs=[hbm, hbm] + [vmem] * 6,
+        in_specs=[hbm] * 8,
         out_specs=vmem,
         scratch_shapes=[
+            pltpu.VMEM((ROWS, XW), jnp.int32),
+            pltpu.VMEM((1, NBLK), jnp.int32),
+            pltpu.VMEM(mirror.shape, bf16),
+            pltpu.VMEM(first.shape, bf16),
+            pltpu.VMEM(twiddle.shape, f32),
+            pltpu.VMEM(last.shape, bf16),
+            dma((6,)),
             pltpu.VMEM((6 * MODES, KZ), bf16),
             pltpu.VMEM((4, 512, 2 * HALF), bf16),
             pltpu.VMEM((2, 2, 2 * LANES, 2 * HALF), bf16),

time: 41.7 us -> 40.7 us (0.976)
  Pallas kernels: 41 us -> 40 us
    pallas_call x1, Pallas kernels: 41 us -> 40 us  [run(): pl.pallas_call(kernel, out_shape=pltpu.VMEM((6, 128), f32), in_specs=[hbm...]
where the time goes in v8:
time: 40.7 us; the launch traced here: 40.6 us
  Pallas kernels  40 us (98%)
  local copies, waits for them, and re-layouts  0.58 us (1%)
    pallas_call x1, Pallas kernels, run(): pl.pallas_call(kernel, out_shape=pltpu.VMEM((6, 128), f32), in_specs=[hbm...  40 us

profile of v8, /device:TPU:1, one launch (start us, length us, event | category | flops | bytes accessed | tf_op | source)
XLA Modules:
  0.0 40.6 jit_solution(14503694621291356708)
XLA Ops:
  0.0 40.0 %shard_map.82 = f32[6,128]{1,0:T(8,128)S(1)} custom-call(bf16[240,7680]{1,0:T(8,128)(2,1)} %bitcast.4, bf16[4,512,2048]{2,1,0:T(8,128)(2,1)} %constant.10.clone.tab_hbm, s32[16,2048]{1,0:T(8,128)} %lab_hbm.1, s32[1,128]{1,0:T(1,128)} %bitcast.5, bf16[2,256,128]{2,1,0:T(8,128)(2,1)} %constant.11.clone.mirror_hbm, bf16[512,512]{1,0:T(8,128)(2,1)} %constant.12.clone.first_hbm, ...), custom_call_target="tpu_custom_call" | custom-call | tf_op jit(solution)/shard_map/pallas_call | solution.py:371
  40.0 0.6 %copy.9 = f32[6,1,128]{2,1,0:T(1,128)} copy(f32[6,1,128]{2,0,1:T(8,128)S(1)} %bitcast.3) | data formatting | bytes 6144 | tf_op jit(solution)/shard_map/reshape | solution.py:442

commit v9 on v8

--- a/solution.py
+++ b/solution.py
@@ -266,15 +266,7 @@
 
     lax.fori_loop(1, ND, greet, 0)
 
-    for small in smalls[:3]:
-        small.wait()
-    places = jnp.broadcast_to(place_ref[...], (16, LB))
-    for i in range(XW // LB):
-        cols = slice(i * LB, (i + 1) * LB)
-        lab = lab_ref[:, cols]
-        targets[:, cols] = jnp.take_along_axis(places, lab >> 7, axis=1) * LB + (lab & 127)
-    acc[...] = jnp.zeros_like(acc)
-
+    smalls[0].wait()
     load.wait()
     for za in order:
         loads[za].start()
@@ -305,8 +297,14 @@
         own = pltpu.make_async_copy(msg.at[pair, me], recv.at[pair, me], own_sem.at[pair])
         own.start()
         owns.append(own)
-    for small in smalls[3:]:
+    for small in smalls[1:]:
         small.wait()
+    places = jnp.broadcast_to(place_ref[...], (16, LB))
+    for i in range(XW // LB):
+        cols = slice(i * LB, (i + 1) * LB)
+        lab = lab_ref[:, cols]
+        targets[:, cols] = jnp.take_along_axis(places, lab >> 7, axis=1) * LB + (lab & 127)
+    acc[...] = jnp.zeros_like(acc)
 
     for pair in range(2):
         owns[pair].wait()

time: 40.7 us -> 40.5 us (level)
  no operation moved by 1% of the time
where the time goes in v9:
time: 40.5 us; the launch traced here: 40.4 us
  Pallas kernels  39.8 us (98%)
  local copies, waits for them, and re-layouts  0.58 us (1%)
    pallas_call x1, Pallas kernels, run(): pl.pallas_call(kernel, out_shape=pltpu.VMEM((6, 128), f32), in_specs=[hbm...  39.8 us

profile of v9, /device:TPU:1, one launch (start us, length us, event | category | flops | bytes accessed | tf_op | source)
XLA Modules:
  0.0 40.4 jit_solution(7470583385351379513)
XLA Ops:
  0.0 39.8 %shard_map.82 = f32[6,128]{1,0:T(8,128)S(1)} custom-call(bf16[240,7680]{1,0:T(8,128)(2,1)} %bitcast.4, bf16[4,512,2048]{2,1,0:T(8,128)(2,1)} %constant.10.clone.tab_hbm, s32[16,2048]{1,0:T(8,128)} %lab_hbm.1, s32[1,128]{1,0:T(1,128)} %bitcast.5, bf16[2,256,128]{2,1,0:T(8,128)(2,1)} %constant.11.clone.mirror_hbm, bf16[512,512]{1,0:T(8,128)(2,1)} %constant.12.clone.first_hbm, ...), custom_call_target="tpu_custom_call" | custom-call | tf_op jit(solution)/shard_map/pallas_call | solution.py:369
  39.8 0.6 %copy.9 = f32[6,1,128]{2,1,0:T(1,128)} copy(f32[6,1,128]{2,0,1:T(8,128)S(1)} %bitcast.3) | data formatting | bytes 6144 | tf_op jit(solution)/shard_map/reshape | solution.py:440
